TPU v7x, 128 devices: a whole 4x4x4 slice. The times are simulated.
128 devices in a mesh: dp: 16 (over z, y), fsdp: 8 (over x, core).
Axes of the slice: x: 4, y: 4, z: 4, core: 2. Of those that a mesh axis runs over, the one named last changes fastest.
Arguments:
- queries: bfloat16 [49152, 2048], P(('dp', 'fsdp')), may hold values from -16 to 16
- passages: bfloat16 [49152, 2048], P(('dp', 'fsdp')), may hold values from -16 to 16
- weight: bfloat16 [2048, 2048], P('fsdp'), may hold values from -0.125 to 0.125
- bank: bfloat16 [1024, 128, 2048], P(('dp', 'fsdp')), may hold values from -6 to 6
- neg_ids: int32 [128, 16], P(('dp', 'fsdp')), may hold values from 0 to 1023, as said below
- block_home: int32 [1024], replicated, may hold values from 0 to 1023, as said below
Outputs:
- loss: float32 [], replicated
- grad_weight: float32 [2048, 2048], P(('dp', 'fsdp'))
- grad_queries: bfloat16 [49152, 2048], P(('dp', 'fsdp'))
- grad_passages: bfloat16 [49152, 2048], P(('dp', 'fsdp'))
Inputs may be any that keep to these rules, and one draw needn't show every extreme that they name: `block_home`: A permutation of the slots; block b is held on a device whose fsdp index is b % 8. `neg_ids`: A group's 16 blocks are distinct and all held on devices of the group's own fsdp index; at most 2 of them on one device, and in every group some device holds exactly 2; in each fsdp index one device holds 2 of every group's blocks.
All inputs are finite; a program needn't handle non-finite values.
Results may differ from a plain program's by a relative error of at most 0.012.
The roundings to bfloat16 on the way count: a program that leaves them out, or rounds other values in their place, can miss the bound.
Values may be sent and summed in bfloat16 or wider, within the bound.
A program may use at most 128 MiB of HBM per device.

v0:
```python
import math

import jax
import jax.numpy as jnp
from jax import lax
from jax.sharding import PartitionSpec as P

CAP = 2


SOFTMAX_TEMPER = 0.25


def body(queries, passages, weight, bank, neg_ids, block_home):
    count_q = queries.shape[0]
    slice_width = weight.shape[1]
    logit_scale = 1.0 / (SOFTMAX_TEMPER * math.sqrt(slice_width))
    full_weight = lax.all_gather(weight, "fsdp", axis=0, tiled=True)
    hidden = jnp.concatenate([queries, passages], axis=0)
    embedded = jnp.dot(hidden, full_weight, preferred_element_type=jnp.float32).astype(jnp.bfloat16)
    emb_q = embedded[:count_q]
    emb_p = embedded[count_q:]
    n_dp = lax.axis_size("dp")
    n_fsdp = lax.axis_size("fsdp")
    per_dev = bank.shape[0]
    block_rows = bank.shape[1]
    named = neg_ids.shape[1]
    slots = block_home[neg_ids[0]]
    owner = slots // per_dev // n_fsdp
    local = slots % per_dev
    order = jnp.arange(named)
    earlier = (owner[None, :] == owner[:, None]) & (order[None, :] < order[:, None])
    rank = jnp.sum(earlier.astype(jnp.int32), axis=1)
    peers = jnp.arange(n_dp)
    places = jnp.arange(CAP)
    hit = (owner[:, None, None] == peers[None, :, None]) & (
        rank[:, None, None] == places[None, None, :]
    )
    request = jnp.sum(jnp.where(hit, local[:, None, None] + 1, 0), axis=0) - 1
    asked = lax.all_to_all(request, "dp", split_axis=0, concat_axis=0, tiled=True)
    valid = asked >= 0
    picked = jnp.take(bank, jnp.clip(asked, 0, per_dev - 1), axis=0)
    picked = jnp.where(valid[:, :, None, None], picked, jnp.zeros_like(picked))
    replies = lax.all_to_all(picked, "dp", split_axis=0, concat_axis=0, tiled=True)
    replies = replies.reshape(n_dp * CAP, block_rows, slice_width)
    negs = jnp.take(replies, owner * CAP + rank, axis=0).reshape(named * block_rows, slice_width)
    inner = jnp.dot(emb_q, emb_p.T, preferred_element_type=jnp.float32) * logit_scale
    outer = jnp.dot(emb_q, negs.T, preferred_element_type=jnp.float32) * logit_scale
    scores = jnp.concatenate([inner, outer], axis=1)
    top = jnp.max(scores, axis=1, keepdims=True)
    expo = jnp.exp(scores - top)
    total = jnp.sum(expo, axis=1, keepdims=True)
    lse = top[:, 0] + jnp.log(total[:, 0])
    loss_local = jnp.sum(lse - jnp.diagonal(inner))
    target = jnp.concatenate(
        [
            jnp.eye(count_q, dtype=jnp.float32),
            jnp.zeros((count_q, named * block_rows), jnp.float32),
        ],
        axis=1,
    )
    grad_s = ((expo / total - target) * logit_scale).astype(jnp.bfloat16)
    grad_in = grad_s[:, :count_q]
    grad_out = grad_s[:, count_q:]
    query_gradient = (
        jnp.dot(grad_in, emb_p, preferred_element_type=jnp.float32)
        + jnp.dot(grad_out, negs, preferred_element_type=jnp.float32)
    ).astype(jnp.bfloat16)
    grad_p = lax.dot_general(
        grad_in, emb_q, (((0,), (0,)), ((), ())), preferred_element_type=jnp.float32
    ).astype(jnp.bfloat16)
    grad_rows = jnp.concatenate([query_gradient, grad_p], axis=0)
    back = lax.dot_general(
        grad_rows, full_weight, (((1,), (1,)), ((), ())), preferred_element_type=jnp.float32
    ).astype(jnp.bfloat16)
    devices_all = n_dp * n_fsdp
    loss = lax.psum(loss_local, ("dp", "fsdp")) / (count_q * devices_all)
    grad_weight = lax.psum_scatter(
        lax.dot_general(
            hidden, grad_rows, (((0,), (0,)), ((), ())), preferred_element_type=jnp.float32
        ),
        ("dp", "fsdp"),
        scatter_dimension=0,
        tiled=True,
    )
    return (loss, grad_weight, back[:count_q], back[count_q:])


def solution(mesh):
    return jax.shard_map(
        body,
        mesh=mesh,
        in_specs=(
            P(("dp", "fsdp"), None),
            P(("dp", "fsdp"), None),
            P("fsdp", None),
            P(("dp", "fsdp"), None, None),
            P(("dp", "fsdp"), None),
            P(),
        ),
        out_specs=(P(), P(("dp", "fsdp"), None), P(("dp", "fsdp"), None), P(("dp", "fsdp"), None)),
        check_vma=False,
    )
```

profile of v0, /device:TPU:0, one launch (start us, length us, event | category | flops | bytes accessed | tf_op | source)
XLA Modules:
  0.0 1019.6 jit_solution(12237774878966398095)
XLA Ops:
  9.6 8.1 all-to-all-start
  18.5 6.7 all-to-all-done
  25.7 10.2 %gather_fusion.1 = bf16[32,128,2048]{2,1,0:T(8,128)(2,1)} fusion(bf16[8,128,2048]{2,1,0:T(8,128)(2,1)} %param.9, s32[1024]{0:T(1024)S(1)} %pad_clamp_fusion.1), kind=kCustom, calls=%fused_computation.1 | custom fusion | bytes 33554560 | tf_op jit(solution)/shard_map/jit(_take)/gather | solution.py:42
  35.9 14.4 %select_select_fusion = bf16[16,2,128,2048]{3,2,1,0:T(8,128)(2,1)} fusion(bf16[16,2,128,2048]{3,2,1,0:T(8,128)(2,1)} %bitcast.42, pred[16,2]{1,0:T(8,128)(4,1)S(1)} %copy.38, pred[16,2]{1,0:T(8,128)(4,1)S(1)} %copy.36), kind=kLoop, calls=%fused_computation.4 | loop fusion | flops 16777216 | bytes 33554496 | tf_op jit(solution)/shard_map/jit(_where)/select_n | solution.py:43
  50.3 5.3 all-to-all-start.1
  55.8 1.2 constant_dynamic-update-slice_fusion.1
  57.3 1.3 constant_dynamic-update-slice_fusion
  58.6 12.9 %all-gather.2.cloned.1.call-done = bf16[2048,2048]{1,0:T(8,128)(2,1)} async-done(((bf16[256,2048]{1,0:T(8,128)(2,1)}), bf16[2048,2048]{1,0:T(8,128)(2,1)}) %all-gather.2.cloned.1.call-update) | async-done | bytes 8388624 | tf_op jit(solution)/shard_map/all_gather | solution.py:18
  71.5 10.0 convolution_convert_fusion.1
  81.6 1.0 fusion.23
  83.5 215.9 %all-to-all-done.1 = bf16[16,2,128,2048]{3,2,1,0:T(8,128)(2,1)} async-done(((bf16[16,2,128,2048]{3,2,1,0:T(8,128)(2,1)}), bf16[16,2,128,2048]{3,2,1,0:T(8,128)(2,1)}, u32[]{:S(2)}, u32[]{:S(2)}) %all-to-all-start.1) | async-done | bytes 16777248 | tf_op jit(solution)/shard_map/all_to_all | solution.py:44
  299.4 10.5 %gather_fusion.2 = bf16[16,128,2048]{2,1,0:T(8,128)(2,1)} fusion(bf16[32,128,2048]{2,1,0:T(8,128)(2,1)} %bitcast.8, s32[1024]{0:T(1024)S(1)} %pad_clamp_fusion), kind=kCustom, calls=%fused_computation.2 | custom fusion | bytes 16777280 | tf_op jit(solution)/shard_map/jit(_take)/gather | solution.py:46
  309.9 7.4 bitcast_select_fusion
  317.3 6.5 fusion.24
  324.5 1.1 multiply_convert_fusion
  325.6 1.6 copy-done.2
  327.2 3.4 fusion.3
  330.6 1.0 convolution_convert_fusion.2
  332.8 12.2 %fusion.2 = f32[2048,2048]{1,0:T(8,128)} fusion(bf16[768,2048]{1,0:T(8,128)(2,1)} %constant_dynamic-update-slice_fusion, bf16[384,2048]{1,0:T(8,128)(2,1)S(1)} %convolution_convert_fusion.2, bf16[384,2048]{1,0:T(8,128)(2,1)S(1)} %add_convert_fusion), kind=kOutput, calls=%fused_computation.16 | convolution fusion | flops 6448742400 | bytes 23068672 | tf_op jit(solution)/shard_map/dot_general | solution.py:79
  345.0 3.5 gather_fusion.3
  349.1 66.8 %psum.7 = f32[]{:T(128)} all-reduce(f32[]{:T(128)} %subtract_reduce_fusion), channel_id=1, replica_groups=mesh['dp'=16,'fsdp'=8] {'dp','fsdp'}, use_global_device_ids=true, to_apply=%region_6.7 | all-reduce | flops 1 | bytes 8 | tf_op jit(solution)/shard_map/psum | solution.py:77
  416.6 9.7 convolution_convert_fusion
  426.2 1.9 fusion.22
  428.1 583.6 %reduce-scatter.2.cloned.1.call-done = f32[16,2048]{1,0:T(8,128)} async-done(((f32[2048,2048]{1,0:T(8,128)}), f32[16,2048]{1,0:T(8,128)}) %reduce-scatter.2.cloned.1.call-update) | async-done | bytes 131088 | tf_op jit(solution)/shard_map/reduce_scatter | solution.py:78
  (49 shorter events, 7.3 us)
Async XLA Ops:
  7.2 0.7 copy-start
  9.6 15.6 %all-to-all-start = ((s32[16,1,2]{2,1,0:T(1,128)}), s32[16,1,2]{2,1,0:T(1,128)S(1)}, u32[]{:S(2)}, u32[]{:S(2)}) async-start(s32[16,1,2]{2,1,0:T(1,128)} %copy.34), calls=%async_computation | async-start | bytes 16384 | tf_op jit(solution)/shard_map/all_to_all | solution.py:40
  17.7 53.8 %all-gather.2.cloned.1.call-start = ((), (), s32[]{:S(2)}) async-start(), calls=%async_computation.3 | async-start | bytes 9437184 | tf_op jit(solution)/shard_map/all_gather | solution.py:18
  50.3 5.5 copy-start.3
  50.3 249.0 %all-to-all-start.1 = ((bf16[16,2,128,2048]{3,2,1,0:T(8,128)(2,1)}), bf16[16,2,128,2048]{3,2,1,0:T(8,128)(2,1)}, u32[]{:S(2)}, u32[]{:S(2)}) async-start(bf16[16,2,128,2048]{3,2,1,0:T(8,128)(2,1)} %select_select_fusion), calls=%async_computation.1 | async-start | bytes 33554432 | tf_op jit(solution)/shard_map/all_to_all | solution.py:44
  55.6 1.7 copy-start.4
  55.6 956.1 %reduce-scatter.2.cloned.1.call-start = ((), (), s32[]{:S(2)}) async-start(), calls=%async_computation.4 | async-start | bytes 16908288 | tf_op jit(solution)/shard_map/reduce_scatter | solution.py:78
  81.6 1.7 copy-start.5
  323.8 3.4 copy-start.2
  327.2 3.4 copy-start.6
  331.6 1.1 copy-start.7
  416.5 595.1 %copy-start.1 = (s32[1024]{0:T(1024)S(1)}, s32[1024]{0:T(1024)}, u32[]{:S(2)}) copy-start(s32[1024]{0:T(1024)} %param.11) | copy-start | bytes 12292
Sparse Core Ops, SparseCore 0:
  20.3 51.2 all-gather.1
  345.1 666.4 reduce-scatter.1
where the time goes:
time: 1020 us
  waiting for transfers between devices  820 us (80%)
  blocking collectives  66.8 us (7%)
  matrix products  44.8 us (4%)
  local copies, waits for them, and re-layouts  33.3 us (3%)
  other arithmetic  25.4 us (2%)
  between operations  16 us (2%)
  starting transfers between devices  13.5 us (1%)
    reduce_scatter x1, waiting for transfers between devices, body(): lax.psum_scatter(lax.dot_general(hidden, grad_rows, (((0,), (0,)), ((), (...  584 us
    all_to_all x1, waiting for transfers between devices, body(): lax.all_to_all(picked, 'dp', split_axis=0, concat_axis=0, tiled=True)  216 us
    psum x1, blocking collectives, body(): loss = lax.psum(loss_local, ('dp', 'fsdp')) / (count_q * devices_all)  66.8 us
  transfers between devices with their start and end apart: 4, of which 4 were waited for; matrix products, arithmetic and copies ran while one was open for 5% of the time, Pallas kernels for 0%

commit v1 on v0

--- a/solution.py
+++ b/solution.py
@@ -3,12 +3,271 @@
 import jax
 import jax.numpy as jnp
 from jax import lax
+from jax.experimental import pallas as pl
+from jax.experimental.pallas import tpu as pltpu
 from jax.sharding import PartitionSpec as P
 
 CAP = 2
 
 
 SOFTMAX_TEMPER = 0.25
+
+MESH = pl.DeviceIdType.MESH
+RING = 4
+ROWS = 16
+PARTS = (
+    (0, 768, 384, (2, 1, 0)),
+    (768, 640, 384, (1, 0, 2)),
+    (1408, 640, 384, (0, 2, 1)),
+)
+
+
+def position():
+    dp = lax.axis_index("dp")
+    fsdp = lax.axis_index("fsdp")
+    return (lax.div(dp, RING), lax.rem(dp, RING), lax.div(fsdp, 2)), lax.rem(fsdp, 2)
+
+
+def device(coords, core):
+    return (coords[0] * RING + coords[1], coords[2] * 2 + core)
+
+
+def shifted(coords, axis, by):
+    moved = list(coords)
+    moved[axis] = lax.rem(coords[axis] + by + RING, RING)
+    return tuple(moved)
+
+
+def greet(targets):
+    barrier = pltpu.get_barrier_semaphore()
+    for target in targets:
+        pl.semaphore_signal(barrier, inc=1, device_id=target, device_id_type=MESH)
+    pl.semaphore_wait(barrier, len(targets))
+
+
+def remote(src, dst, send, recv, target):
+    return pltpu.make_async_remote_copy(
+        src_ref=src, dst_ref=dst, send_sem=send, recv_sem=recv, device_id=target, device_id_type=MESH
+    )
+
+
+def pick(rank, spot, index, columns):
+    return tuple(index if i == spot else slice(None) for i in range(rank)) + (slice(None), columns)
+
+
+def reduce_kernel(share_ref, loss_ref, out_ref, total_ref, *scratch):
+    coords, core = position()
+    sibling = device(coords, 1 - core)
+    near = [[device(shifted(coords, a, by), core) for by in (1, 3)] for a in range(3)]
+    far = [device(shifted(coords, a, 2), core) for a in range(3)]
+    greet([sibling] + [d for pair in near for d in pair] + far)
+
+    count = len(PARTS)
+    paired = scratch[0]
+    sums = [[scratch[1 + 3 * p + k] for k in range(3)] for p in range(count)]
+    base = 1 + 3 * count
+    passing = [[[scratch[base + 6 * p + 2 * k + d] for d in range(2)] for k in range(3)] for p in range(count)]
+    base += 6 * count
+    arriving = [[scratch[base + 3 * p + k] for k in range(3)] for p in range(count)]
+    base += 3 * count
+    loss_buf, send0, recv0, send, recv, loss_send, loss_recv = scratch[base:]
+
+    started = []
+
+    def go(copy):
+        copy.start()
+        started.append(copy)
+        return copy
+
+    first = []
+    for p, (lo, width, cut, order) in enumerate(PARTS):
+        columns = pl.ds(lo, width)
+        first.append(
+            go(
+                remote(
+                    share_ref.at[:, :, :, 1 - core, :, columns],
+                    paired.at[:, :, :, :, columns],
+                    send0.at[p],
+                    recv0.at[p],
+                    sibling,
+                )
+            )
+        )
+
+    loss_buf[0, pl.ds(core, 1)] = loss_ref[...][None]
+    pair_loss = go(
+        remote(loss_buf.at[0, core], loss_buf.at[0, core], loss_send.at[0, 0], loss_recv.at[0, 0], sibling)
+    )
+
+    def loss_step(level, copies, slots):
+        for copy in copies:
+            copy.wait_recv()
+        value = loss_buf[level, 0]
+        for s in range(1, slots):
+            value = value + loss_buf[level, s]
+        return value
+
+    def loss_send_axis(level, axis, value):
+        mine = coords[axis]
+        loss_buf[level, pl.ds(mine, 1)] = value[None]
+        copies = []
+        for n, target in enumerate((near[axis][0], near[axis][1], far[axis])):
+            copies.append(
+                go(
+                    remote(
+                        loss_buf.at[level, mine],
+                        loss_buf.at[level, mine],
+                        loss_send.at[level, n],
+                        loss_recv.at[level, n],
+                        target,
+                    )
+                )
+            )
+        return copies
+
+    def halves(width, cut):
+        return pl.ds(0, cut), pl.ds(cut, width - cut)
+
+    def begin(p, k):
+        lo, width, cut, order = PARTS[p]
+        axis = order[k]
+        rest = sorted(order[k:])
+        spot, rank = rest.index(axis), len(rest)
+        mine = coords[axis]
+        both = halves(width, cut)
+        source = sums[p][k]
+        moves = {"far": [], "near": []}
+        for d in range(2):
+            moves["far"].append(
+                go(
+                    remote(
+                        source.at[pick(rank, spot, lax.rem(mine + 2, RING), both[d])],
+                        passing[p][k][d],
+                        send.at[p, k, d],
+                        recv.at[p, k, d],
+                        near[axis][d],
+                    )
+                )
+            )
+        for d in range(2):
+            by = 1 if d == 0 else 3
+            moves["near"].append(
+                go(
+                    remote(
+                        source.at[pick(rank, spot, lax.rem(mine + by, RING), both[1 - d])],
+                        arriving[p][k].at[(d,) + pick(rank - 1, -1, 0, both[1 - d])],
+                        send.at[p, k, 2 + d],
+                        recv.at[p, k, 2 + d],
+                        near[axis][d],
+                    )
+                )
+            )
+        return moves
+
+    def relay(p, k, moves):
+        lo, width, cut, order = PARTS[p]
+        axis = order[k]
+        rest = sorted(order[k:])
+        spot, rank = rest.index(axis), len(rest)
+        mine = coords[axis]
+        both = halves(width, cut)
+        source = sums[p][k]
+        for d in range(2):
+            by = 1 if d == 0 else 3
+            moves["far"][d].wait_recv()
+            where = pick(rank, spot, lax.rem(mine + by, RING), both[d])
+            mixed = source[where].astype(jnp.float32) + passing[p][k][d][...].astype(jnp.float32)
+            source[where] = mixed.astype(jnp.bfloat16)
+            moves["near"].append(
+                go(
+                    remote(
+                        source.at[where],
+                        arriving[p][k].at[(d,) + pick(rank - 1, -1, 0, both[d])],
+                        send.at[p, k, 4 + d],
+                        recv.at[p, k, 4 + d],
+                        near[axis][d],
+                    )
+                )
+            )
+
+    def finish(p, k, moves):
+        lo, width, cut, order = PARTS[p]
+        axis = order[k]
+        rest = sorted(order[k:])
+        spot, rank = rest.index(axis), len(rest)
+        for copy in moves["near"]:
+            copy.wait_recv()
+        own = sums[p][k][pick(rank, spot, coords[axis], slice(None))].astype(jnp.float32)
+        done = own + arriving[p][k][0].astype(jnp.float32) + arriving[p][k][1].astype(jnp.float32)
+        if k < 2:
+            sums[p][k + 1][...] = done.astype(jnp.bfloat16)
+        else:
+            out_ref[:, pl.ds(lo, width)] = done
+
+    moves = []
+    for p, (lo, width, cut, order) in enumerate(PARTS):
+        columns = pl.ds(lo, width)
+        first[p].wait_recv()
+
+        @pl.loop(0, RING)
+        def _(i):
+            a = share_ref[i, :, :, core, :, columns].astype(jnp.float32)
+            b = paired[i, :, :, :, columns].astype(jnp.float32)
+            sums[p][0][i] = (a + b).astype(jnp.bfloat16)
+
+        moves.append(begin(p, 0))
+
+    value = loss_step(0, [pair_loss], 2)
+    for k in range(3):
+        loss_copies = loss_send_axis(1 + k, k, value)
+        for p in range(count):
+            relay(p, k, moves[p])
+        for p in range(count):
+            finish(p, k, moves[p])
+            if k < 2:
+                moves[p] = begin(p, k + 1)
+        value = loss_step(1 + k, loss_copies, RING)
+    total_ref[...] = value
+    for copy in started:
+        copy.wait_send()
+
+
+def reduce_gradient(share, loss):
+    width = share.shape[1]
+    share = share.reshape(RING, RING, RING, 2, ROWS, width)
+    scratch = [pltpu.VMEM((RING, RING, RING, ROWS, width), jnp.bfloat16)]
+    for _, columns, _, _ in PARTS:
+        scratch += [pltpu.VMEM((RING,) * (3 - k) + (ROWS, columns), jnp.bfloat16) for k in range(3)]
+    for _, columns, cut, _ in PARTS:
+        for k in range(3):
+            for part in (cut, columns - cut):
+                scratch.append(pltpu.VMEM((RING,) * (2 - k) + (ROWS, part), jnp.bfloat16))
+    for _, columns, _, _ in PARTS:
+        scratch += [pltpu.VMEM((2,) + (RING,) * (2 - k) + (ROWS, columns), jnp.bfloat16) for k in range(3)]
+    scratch += [
+        pltpu.VMEM((4, RING, 8, 128), jnp.float32),
+        pltpu.SemaphoreType.DMA((len(PARTS),)),
+        pltpu.SemaphoreType.DMA((len(PARTS),)),
+        pltpu.SemaphoreType.DMA((len(PARTS), 3, 6)),
+        pltpu.SemaphoreType.DMA((len(PARTS), 3, 6)),
+        pltpu.SemaphoreType.DMA((4, 3)),
+        pltpu.SemaphoreType.DMA((4, 3)),
+    ]
+    vmem = pl.BlockSpec(memory_space=pltpu.VMEM)
+    return pl.pallas_call(
+        reduce_kernel,
+        out_shape=(
+            jax.ShapeDtypeStruct((ROWS, width), jnp.float32),
+            jax.ShapeDtypeStruct((8, 128), jnp.float32),
+        ),
+        in_specs=[vmem, vmem],
+        out_specs=(vmem, vmem),
+        scratch_shapes=scratch,
+        compiler_params=pltpu.CompilerParams(
+            collective_id=2, has_side_effects=True, vmem_limit_bytes=48 * 1024 * 1024
+        ),
+        name="reduce_gradient",
+    )(share, loss)
 
 
 def body(queries, passages, weight, bank, neg_ids, block_home):
@@ -74,15 +333,11 @@
         grad_rows, full_weight, (((1,), (1,)), ((), ())), preferred_element_type=jnp.float32
     ).astype(jnp.bfloat16)
     devices_all = n_dp * n_fsdp
-    loss = lax.psum(loss_local, ("dp", "fsdp")) / (count_q * devices_all)
-    grad_weight = lax.psum_scatter(
-        lax.dot_general(
-            hidden, grad_rows, (((0,), (0,)), ((), ())), preferred_element_type=jnp.float32
-        ),
-        ("dp", "fsdp"),
-        scatter_dimension=0,
-        tiled=True,
-    )
+    share = lax.dot_general(
+        hidden, grad_rows, (((0,), (0,)), ((), ())), preferred_element_type=jnp.float32
+    ).astype(jnp.bfloat16)
+    grad_weight, losses = reduce_gradient(share, jnp.full((8, 128), loss_local, jnp.float32))
+    loss = losses[0, 0] / (count_q * devices_all)
     return (loss, grad_weight, back[:count_q], back[count_q:])
 
 

time: 1020 us -> 407 us (0.40)
  waiting for transfers between devices: 820 us -> 233 us
  blocking collectives: 66.8 us -> 0 us
  Pallas kernels: 0 us -> 42.6 us
    reduce_scatter x1 -> x0, waiting for transfers between devices: 584 us -> none  [body(): lax.psum_scatter(lax.dot_general(hidden, grad_rows, (((0,), (0,)), ((), (...]
    psum x1 -> x0, blocking collectives: 66.8 us -> none  [body(): loss = lax.psum(loss_local, ('dp', 'fsdp')) / (count_q * devices_all)]
    pallas_call x0 -> x1, Pallas kernels: none -> 42.6 us  [reduce_gradient(): pl.pallas_call(reduce_kernel, out_shape=(jax.ShapeDtypeStruct((ROWS, widt...]
  transfers between devices with their start and end apart: 4 -> 3, of which waited for: 4 -> 3; matrix products, arithmetic and copies ran while one was open for 5% -> 10% of each run, Pallas kernels for 0% -> 0%
where the time goes in v1:
time: 407 us; the launch traced here: 406 us
  waiting for transfers between devices  233 us (57%)
  Pallas kernels  42.6 us (10%)
  matrix products  41.1 us (10%)
  local copies, waits for them, and re-layouts  34.9 us (9%)
  other arithmetic  25.6 us (6%)
  between operations  16 us (4%)
  starting transfers between devices  13.4 us (3%)
    all_to_all x1, waiting for transfers between devices, body(): lax.all_to_all(picked, 'dp', split_axis=0, concat_axis=0, tiled=True)  212 us
    pallas_call x1, Pallas kernels, reduce_gradient(): pl.pallas_call(reduce_kernel, out_shape=(jax.ShapeDtypeStruct((ROWS, widt...  42.6 us
    select_n x1, other arithmetic, body(): picked = jnp.where(valid[:, :, None, None], picked, jnp.zeros_like(picked))  14.4 us
    all_gather x1, waiting for transfers between devices, body(): full_weight = lax.all_gather(weight, 'fsdp', axis=0, tiled=True)  12.9 us
    dot_general x1, matrix products, body(): lax.dot_general(hidden, grad_rows, (((0,), (0,)), ((), ())), preferred_el...  11.2 us
    gather x1, local copies, waits for them, and re-layouts, body(): jnp.take(replies, owner * CAP + rank, axis=0)  10.5 us
    gather x1, local copies, waits for them, and re-layouts, body(): picked = jnp.take(bank, jnp.clip(asked, 0, per_dev - 1), axis=0)  10.2 us
    dot_general x1, matrix products, body(): jnp.dot(hidden, full_weight, preferred_element_type=jnp.float32)  10 us
  transfers between devices with their start and end apart: 3, of which 3 were waited for; matrix products, arithmetic and copies ran while one was open for 10% of the time, Pallas kernels for 0%

profile of v1, /device:TPU:0, one launch (start us, length us, event | category | flops | bytes accessed | tf_op | source)
XLA Modules:
  0.0 406.4 jit_solution(14566857589504763738)
XLA Ops:
  9.6 8.1 %all-to-all-start = ((s32[16,1,2]{2,1,0:T(1,128)}), s32[16,1,2]{2,1,0:T(1,128)S(1)}, u32[]{:S(2)}, u32[]{:S(2)}) async-start(s32[16,1,2]{2,1,0:T(1,128)} %copy.34), calls=%async_computation | async-start | bytes 16384 | tf_op jit(solution)/shard_map/all_to_all | solution.py:299
  18.5 6.7 %all-to-all-done = s32[16,1,2]{2,1,0:T(1,128)S(1)} async-done(((s32[16,1,2]{2,1,0:T(1,128)}), s32[16,1,2]{2,1,0:T(1,128)S(1)}, u32[]{:S(2)}, u32[]{:S(2)}) %all-to-all-start) | async-done | bytes 160 | tf_op jit(solution)/shard_map/all_to_all | solution.py:299
  25.7 10.2 %gather_fusion.1 = bf16[32,128,2048]{2,1,0:T(8,128)(2,1)} fusion(bf16[8,128,2048]{2,1,0:T(8,128)(2,1)} %param.9, s32[1024]{0:T(1024)S(1)} %pad_clamp_fusion.1), kind=kCustom, calls=%fused_computation.1 | custom fusion | bytes 33554560 | tf_op jit(solution)/shard_map/jit(_take)/gather | solution.py:301
  35.9 14.4 %select_select_fusion = bf16[16,2,128,2048]{3,2,1,0:T(8,128)(2,1)} fusion(bf16[16,2,128,2048]{3,2,1,0:T(8,128)(2,1)} %bitcast.44, pred[16,2]{1,0:T(8,128)(4,1)S(1)} %copy.38, pred[16,2]{1,0:T(8,128)(4,1)S(1)} %copy.36), kind=kLoop, calls=%fused_computation.4 | loop fusion | flops 16777216 | bytes 33554496 | tf_op jit(solution)/shard_map/jit(_where)/select_n | solution.py:302
  50.3 5.3 %all-to-all-start.1 = ((bf16[16,2,128,2048]{3,2,1,0:T(8,128)(2,1)}), bf16[16,2,128,2048]{3,2,1,0:T(8,128)(2,1)}, u32[]{:S(2)}, u32[]{:S(2)}) async-start(bf16[16,2,128,2048]{3,2,1,0:T(8,128)(2,1)} %select_select_fusion), calls=%async_computation.1 | async-start | bytes 33554432 | tf_op jit(solution)/shard_map/all_to_all | solution.py:303
  55.8 1.2 constant_dynamic-update-slice_fusion.1
  57.3 1.3 constant_dynamic-update-slice_fusion
  58.6 12.9 %all-gather.2.cloned.1.call-done = bf16[2048,2048]{1,0:T(8,128)(2,1)} async-done(((bf16[256,2048]{1,0:T(8,128)(2,1)}), bf16[2048,2048]{1,0:T(8,128)(2,1)}) %all-gather.2.cloned.1.call-update) | async-done | bytes 8388624 | tf_op jit(solution)/shard_map/all_gather | solution.py:277
  71.5 10.0 %convolution_convert_fusion.2 = bf16[768,2048]{1,0:T(8,128)(2,1)S(1)} fusion(bf16[768,2048]{1,0:T(8,128)(2,1)} %constant_dynamic-update-slice_fusion, bf16[2048,2048]{1,0:T(8,128)(2,1)} %all-gather.2.cloned.1.call-done), kind=kOutput, calls=%fused_computation.11 | convolution fusion | flops 6444023808 | bytes 14680064 | tf_op jit(solution)/shard_map/dot_general | solution.py:279
  81.6 1.0 fusion.22
  83.4 3.5 gather_fusion.3
  86.9 212.4 %all-to-all-done.1 = bf16[16,2,128,2048]{3,2,1,0:T(8,128)(2,1)} async-done(((bf16[16,2,128,2048]{3,2,1,0:T(8,128)(2,1)}), bf16[16,2,128,2048]{3,2,1,0:T(8,128)(2,1)}, u32[]{:S(2)}, u32[]{:S(2)}) %all-to-all-start.1) | async-done | bytes 16777248 | tf_op jit(solution)/shard_map/all_to_all | solution.py:303
  299.3 10.5 %gather_fusion.2 = bf16[16,128,2048]{2,1,0:T(8,128)(2,1)} fusion(bf16[32,128,2048]{2,1,0:T(8,128)(2,1)} %bitcast.8, s32[1024]{0:T(1024)S(1)} %pad_clamp_fusion), kind=kCustom, calls=%fused_computation.2 | custom fusion | bytes 16777280 | tf_op jit(solution)/shard_map/jit(_take)/gather | solution.py:305
  309.9 7.4 %bitcast_select_fusion = bf16[2048,2048]{1,0:T(8,128)(2,1)} fusion(bf16[16,128,2048]{2,1,0:T(8,128)(2,1)} %gather_fusion.2, pred[2048]{0:T(1024)(128)(4,1)S(1)} %broadcast_bitcast_fusion), kind=kLoop, calls=%fused_computation.5 | loop fusion | flops 4194304 | bytes 16779264 | tf_op jit(solution)/shard_map/jit(_take)/select_n | solution.py:305
  317.3 6.5 %fusion.23 = (f32[384]{0:T(512)S(1)}, f32[384,2048]{1,0:T(8,128)S(1)}) fusion(bf16[2048,2048]{1,0:T(8,128)(2,1)} %bitcast_select_fusion, bf16[768,2048]{1,0:T(8,128)(2,1)} %copy-done.5), kind=kOutput, calls=%fused_computation.78 | convolution fusion | flops 3222797824 | bytes 13108736 | tf_op jit(solution)/shard_map/dot_general | solution.py:307
  324.5 1.3 multiply_convert_fusion
  325.8 1.4 copy-done.2
  327.2 3.4 fusion.2
  330.6 1.0 convolution_convert_fusion.3
  331.6 1.0 add_convert_fusion
  332.6 11.2 %convolution_convert_fusion = bf16[2048,2048]{1,0:T(8,128)(2,1)} fusion(bf16[768,2048]{1,0:T(8,128)(2,1)} %constant_dynamic-update-slice_fusion, bf16[384,2048]{1,0:T(8,128)(2,1)S(1)} %convolution_convert_fusion.3, bf16[384,2048]{1,0:T(8,128)(2,1)S(1)} %add_convert_fusion), kind=kOutput, calls=%fused_computation.6 | convolution fusion | flops 6452936704 | bytes 14680064 | tf_op jit(solution)/shard_map/dot_general | solution.py:336
  343.9 6.9 %convolution_convert_fusion.1 = bf16[768,2048]{1,0:T(8,128)(2,1)S(1)} fusion(bf16[2048,2048]{1,0:T(8,128)(2,1)S(1)} %bitcast.47, bf16[384,2048]{1,0:T(8,128)(2,1)S(1)} %convolution_convert_fusion.3, bf16[384,2048]{1,0:T(8,128)(2,1)S(1)} %add_convert_fusion), kind=kOutput, calls=%fused_computation.10 | convolution fusion | flops 6450315264 | bytes 14680064 | tf_op jit(solution)/shard_map/dot_general | solution.py:332
  350.8 1.9 fusion.21
  354.0 42.6 %reduce_gradient.1 = (f32[16,2048]{1,0:T(8,128)S(1)}, f32[8,128]{1,0:T(8,128)S(1)}) custom-call(bf16[4,4,4,2,16,2048]{5,4,3,2,1,0:T(8,128)(2,1)} %bitcast.45, f32[8,128]{1,0:T(8,128)S(1)} %broadcast_in_dim.78.loss_ref), custom_call_target="tpu_custom_call" | custom-call | tf_op jit(solution)/shard_map/reduce_gradient/pallas_call | solution.py:257
  (52 shorter events, 8.0 us)
Async XLA Ops:
  7.2 0.7 copy-start
  9.6 15.6 %all-to-all-start = ((s32[16,1,2]{2,1,0:T(1,128)}), s32[16,1,2]{2,1,0:T(1,128)S(1)}, u32[]{:S(2)}, u32[]{:S(2)}) async-start(s32[16,1,2]{2,1,0:T(1,128)} %copy.34), calls=%async_computation | async-start | bytes 16384 | tf_op jit(solution)/shard_map/all_to_all | solution.py:299
  17.7 53.8 %all-gather.2.cloned.1.call-start = ((), (), s32[]{:S(2)}) async-start(), calls=%async_computation.2 | async-start | bytes 9437184 | tf_op jit(solution)/shard_map/all_gather | solution.py:277
  50.3 5.5 %copy-start.3 = (bf16[384,2048]{1,0:T(8,128)(2,1)S(1)}, bf16[384,2048]{1,0:T(8,128)(2,1)}, u32[]{:S(2)}) copy-start(bf16[384,2048]{1,0:T(8,128)(2,1)} %param.6) | copy-start | bytes 4718596
  50.3 249.0 %all-to-all-start.1 = ((bf16[16,2,128,2048]{3,2,1,0:T(8,128)(2,1)}), bf16[16,2,128,2048]{3,2,1,0:T(8,128)(2,1)}, u32[]{:S(2)}, u32[]{:S(2)}) async-start(bf16[16,2,128,2048]{3,2,1,0:T(8,128)(2,1)} %select_select_fusion), calls=%async_computation.1 | async-start | bytes 33554432 | tf_op jit(solution)/shard_map/all_to_all | solution.py:303
  55.6 1.7 copy-start.4
  81.6 1.6 copy-start.5
  323.8 3.4 copy-start.2
  327.2 3.4 copy-start.6
  331.6 12.2 %slice-start = ((s8[8388608]{0:T(1024)(128)(4,1)}), s8[4194304]{0:T(1024)(128)(4,1)S(1)}, s32[]{:S(2)}) async-start(s8[8388608]{0:T(1024)(128)(4,1)} %bitcast.46), calls=%async_computation.3 | async-start | bytes 8388608
  332.6 11.3 %slice-start.1 = ((s8[8388608]{0:T(1024)(128)(4,1)}), s8[4194304]{0:T(1024)(128)(4,1)S(1)}, s32[]{:S(2)}) async-start(s8[8388608]{0:T(1024)(128)(4,1)} %bitcast.46), calls=%async_computation.4 | async-start | bytes 8388608
  354.0 44.5 %copy-start.1 = (s32[1024]{0:T(1024)S(1)}, s32[1024]{0:T(1024)}, u32[]{:S(2)}) copy-start(s32[1024]{0:T(1024)} %param.11) | copy-start | bytes 12292
Sparse Core Ops, SparseCore 0:
  20.3 51.2 all-gather.1

commit v2 on v1

--- a/solution.py
+++ b/solution.py
@@ -6,9 +6,6 @@
 from jax.experimental import pallas as pl
 from jax.experimental.pallas import tpu as pltpu
 from jax.sharding import PartitionSpec as P
-
-CAP = 2
-
 
 SOFTMAX_TEMPER = 0.25
 
@@ -270,75 +267,446 @@
     )(share, loss)
 
 
+def ring_position():
+    coords, core = position()
+    r = coords[0] + core * (coords[1] - coords[0])
+    q = coords[1] + core * (coords[0] - coords[1])
+    return r, q, coords[2], core
+
+
+def ring_device(r, q, x, core):
+    r = lax.rem(r + RING, RING)
+    q = lax.rem(q + RING, RING)
+    x = lax.rem(x + RING, RING)
+    return (r * (RING - (RING - 1) * core) + q * (1 + (RING - 1) * core), x * 2 + core)
+
+
+def gather_kernel(
+    q_ref, p_ref, w_ref, bank_ref, list_ref,
+    blocks_ref, allq_ref, embp_ref, full_ref, lists_ref,
+    w_buf, h_buf, acc, embq, embp, list_buf, local_sem, send, recv,
+):
+    r, q, x, core = ring_position()
+    sibling = ring_device(r, q, x, 1 - core)
+    ring = [ring_device(r + by, q, x, core) for by in (1, -1)]
+    row = [ring_device(r, q + by, x, core) for by in (1, -1)]
+    row_far = ring_device(r, q + 2, x, core)
+    line = [ring_device(r, q, x + by, core) for by in (1, -1)]
+    rows = q_ref.shape[0]
+    depth = w_ref.shape[0]
+    many = bank_ref.shape[0]
+    own = x * 2 + core
+    other = x * 2 + 1 - core
+
+    def wrap(v):
+        return lax.rem(v + RING, RING)
+
+    local = []
+
+    def keep(src, dst):
+        copy = pltpu.make_async_copy(src, dst, local_sem.at[len(local)])
+        copy.start()
+        local.append(copy)
+        return copy
+
+    started = []
+
+    def go(src, dst, target):
+        n = len(started)
+        copy = remote(src, dst, send.at[n], recv.at[n], target)
+        copy.start()
+        started.append(copy)
+        return copy
+
+    take_q = keep(q_ref, h_buf.at[pl.ds(0, rows)])
+    take_p = keep(p_ref, h_buf.at[pl.ds(rows, rows)])
+    take_w = keep(w_ref, w_buf.at[own])
+    greet([sibling] + ring + row + [row_far] + line)
+
+    cut_w = (pl.ds(0, depth // 2), pl.ds(depth // 2, depth // 2))
+    cut_b = (pl.ds(0, many // 2), pl.ds(many // 2, many // 2))
+    cut_q = (pl.ds(0, rows // 2), pl.ds(rows // 2, rows // 2))
+
+    w_pair = go(w_ref, w_buf.at[own], sibling)
+    w_near = [None, None]
+    b_near = [None, None]
+    for d in range(2):
+        w_near[d] = [go(w_ref.at[cut_w[h]], w_buf.at[own, cut_w[h]], line[d]) for h in (d, 1 - d)]
+    for d in range(2):
+        b_near[d] = [go(bank_ref.at[cut_b[h]], blocks_ref.at[r, cut_b[h]], ring[d]) for h in (d, 1 - d)]
+    list_copies = [
+        go(list_ref.at[wrap(q + by)], list_buf.at[q], target) for by, target in ((1, row[0]), (-1, row[1]), (2, row_far))
+    ]
+    list_buf[pl.ds(q, 1)] = list_ref[pl.ds(q, 1)]
+    keep_b = keep(bank_ref, blocks_ref.at[r])
+
+    def multiply(part, first=False):
+        @pl.loop(0, acc.shape[1] // 512)
+        def _(n):
+            columns = pl.ds(pl.multiple_of(n * 512, 512), 512)
+            term = jnp.dot(
+                h_buf[:, pl.ds(pl.multiple_of(part * depth, depth), depth)],
+                w_buf[part, :, columns],
+                preferred_element_type=jnp.float32,
+            )
+            if first:
+                acc[:, columns] = term
+            else:
+                acc[:, columns] += term
+
+    take_q.wait()
+    take_p.wait()
+    take_w.wait()
+    multiply(own, True)
+    w_pair.wait_recv()
+    multiply(other)
+
+    across = []
+    w_far = [None, None]
+    for n in range(2):
+        for d in range(2):
+            h = d if n == 0 else 1 - d
+            came = wrap(x - 1 + 2 * d) * 2 + core
+            w_near[d][n].wait_recv()
+            if n == 0:
+                w_far[d] = go(w_buf.at[came, cut_w[h]], w_buf.at[came, cut_w[h]], line[d])
+            across.append(go(w_buf.at[came, cut_w[h]], w_buf.at[came, cut_w[h]], sibling))
+    multiply(wrap(x - 1) * 2 + core)
+    multiply(wrap(x + 1) * 2 + core)
+    b_far = [None, None]
+    for d in range(2):
+        came = wrap(r - 1 + 2 * d)
+        b_near[d][0].wait_recv()
+        b_far[d] = go(blocks_ref.at[came, cut_b[d]], blocks_ref.at[came, cut_b[d]], ring[d])
+    for copy in across:
+        copy.wait_recv()
+    multiply(wrap(x - 1) * 2 + 1 - core)
+    multiply(wrap(x + 1) * 2 + 1 - core)
+    across = []
+    last = wrap(x + 2) * 2
+    for d in range(2):
+        w_far[d].wait_recv()
+        across.append(go(w_buf.at[last + core, cut_w[d]], w_buf.at[last + core, cut_w[d]], sibling))
+    multiply(last + core)
+    for copy in across:
+        copy.wait_recv()
+    multiply(last + 1 - core)
+
+    embq[...] = acc[pl.ds(0, rows)].astype(jnp.bfloat16)
+    q_near = [None, None]
+    for d in range(2):
+        q_near[d] = [go(embq.at[cut_q[h]], allq_ref.at[q, cut_q[h]], row[d]) for h in (d, 1 - d)]
+    keep(embq, allq_ref.at[q])
+    embp[...] = acc[pl.ds(rows, rows)].astype(jnp.bfloat16)
+    keep(embp, embp_ref)
+    keep(w_buf, full_ref)
+    for copy in list_copies:
+        copy.wait_recv()
+    lists_ref[...] = list_buf[...]
+    q_far = [None, None]
+    for d in range(2):
+        came = wrap(q - 1 + 2 * d)
+        q_near[d][0].wait_recv()
+        q_far[d] = go(allq_ref.at[came, cut_q[d]], allq_ref.at[came, cut_q[d]], row[d])
+    for d in range(2):
+        b_near[d][1].wait_recv()
+        b_far[d].wait_recv()
+        q_near[d][1].wait_recv()
+        q_far[d].wait_recv()
+    for copy in local[3:]:
+        copy.wait()
+    for copy in started:
+        copy.wait_send()
+
+
+def gather_and_embed(queries, passages, weight, bank, lists):
+    rows, features = queries.shape
+    depth, width = weight.shape
+    parts = features // depth
+    many, block_rows = bank.shape[:2]
+    anywhere = pl.BlockSpec(memory_space=pl.ANY)
+    vmem = pl.BlockSpec(memory_space=pltpu.VMEM)
+    return pl.pallas_call(
+        gather_kernel,
+        out_shape=(
+            jax.ShapeDtypeStruct((RING, many, block_rows, width), jnp.bfloat16),
+            jax.ShapeDtypeStruct((RING, rows, width), jnp.bfloat16),
+            jax.ShapeDtypeStruct((rows, width), jnp.bfloat16),
+            jax.ShapeDtypeStruct((parts, depth, width), jnp.bfloat16),
+            jax.ShapeDtypeStruct(lists.shape, jnp.int32),
+        ),
+        in_specs=[anywhere] * 4 + [vmem],
+        out_specs=(anywhere,) * 4 + (vmem,),
+        scratch_shapes=[
+            pltpu.VMEM((parts, depth, width), jnp.bfloat16),
+            pltpu.VMEM((2 * rows, features), jnp.bfloat16),
+            pltpu.VMEM((2 * rows, width), jnp.float32),
+            pltpu.VMEM((rows, width), jnp.bfloat16),
+            pltpu.VMEM((rows, width), jnp.bfloat16),
+            pltpu.VMEM(lists.shape, jnp.int32),
+            pltpu.SemaphoreType.DMA((7,)),
+            pltpu.SemaphoreType.DMA((28,)),
+            pltpu.SemaphoreType.DMA((28,)),
+        ],
+        compiler_params=pltpu.CompilerParams(
+            collective_id=0, has_side_effects=True, vmem_limit_bytes=40 * 1024 * 1024
+        ),
+        name="gather_and_embed",
+    )(queries, passages, weight, bank, lists)
+
+
+NONE = -1e30
+
+
+def partial_kernel(
+    scale, allq_ref, blocks_ref, embp_ref, index_ref, list_ref,
+    grad_ref, loss_ref,
+    q_buf, x_buf, p_buf, named, prob, score, mixed, own_mixed,
+    far_out, near_out, passing, arriving,
+    far_stat, near_stat, pass_stat, arrive_stat, arrive_far, local_sem, send, recv,
+):
+    r, q, x, core = ring_position()
+    row = [ring_device(r, q + by, x, core) for by in (1, -1)]
+    rows, width = p_buf.shape
+    places = list_ref.shape[1]
+    half = width // 2
+    sides = (pl.ds(0, half), pl.ds(half, half))
+
+    take = [
+        pltpu.make_async_copy(allq_ref, q_buf, local_sem.at[0]),
+        pltpu.make_async_copy(blocks_ref, x_buf, local_sem.at[1]),
+        pltpu.make_async_copy(embp_ref, p_buf, local_sem.at[2]),
+    ]
+    for copy in take:
+        copy.start()
+    greet(row)
+    for copy in take:
+        copy.wait()
+
+    def wrap(v):
+        return lax.rem(v + RING, RING)
+
+    started = []
+
+    def go(src, dst, target):
+        n = len(started)
+        copy = remote(src, dst, send.at[n], recv.at[n], target)
+        copy.start()
+        started.append(copy)
+        return copy
+
+    eye = lax.broadcasted_iota(jnp.int32, (128, 128), 0) == lax.broadcasted_iota(jnp.int32, (128, 128), 1)
+
+    def pack(stat, m, l):
+        for i in range(rows // 128):
+            for n, value in ((0, m), (rows // 128, l)):
+                part = jnp.where(eye, value[i * 128 : (i + 1) * 128], 0.0)
+                stat[pl.ds(n + i, 1)] = jnp.sum(part, axis=0, keepdims=True)
+
+    def unpack(stat, n):
+        parts = []
+        for i in range(rows // 128):
+            line = stat[pl.ds(n * (rows // 128) + i, 1)]
+            parts.append(jnp.sum(jnp.where(eye, line, 0.0), axis=1, keepdims=True))
+        return jnp.concatenate(parts, axis=0)
+
+    def group(g, result):
+        @pl.loop(0, places)
+        def _(k):
+            block = jnp.maximum(index_ref[g, k, 0], 0)
+            named[pl.ds(pl.multiple_of(k * 128, 128), 128)] = x_buf[block]
+
+        @pl.loop(0, places // 2)
+        def _(n):
+            part = pl.ds(pl.multiple_of(n * 256, 256), 256)
+            score[:, part] = scale * lax.dot_general(
+                q_buf[g], named[part], (((1,), (1,)), ((), ())), preferred_element_type=jnp.float32
+            )
+
+        top = jnp.full((rows, 128), NONE, jnp.float32)
+        for k in range(places):
+            valid = list_ref[g, pl.ds(k, 1)] >= 0
+            top = jnp.maximum(top, jnp.where(valid, score[:, k * 128 : (k + 1) * 128], NONE))
+        m = jnp.max(top, axis=1, keepdims=True)
+        total = jnp.zeros((rows, 128), jnp.float32)
+        for k in range(places):
+            valid = list_ref[g, pl.ds(k, 1)] >= 0
+            e = jnp.where(valid, jnp.exp(score[:, k * 128 : (k + 1) * 128] - m), 0.0)
+            total = total + e
+            prob[:, k * 128 : (k + 1) * 128] = e.astype(jnp.bfloat16)
+        l = jnp.sum(total, axis=1, keepdims=True)
+
+        @pl.loop(0, width // 512)
+        def _(n):
+            part = pl.ds(pl.multiple_of(n * 512, 512), 512)
+            result[:, part] = jnp.dot(prob[...], named[:, part], preferred_element_type=jnp.float32)
+
+        return m, l
+
+    m, l = group(wrap(q + 2), mixed)
+    pack(far_stat, m, l)
+    far = []
+    for d in range(2):
+        far_out[d] = mixed[:, sides[d]].astype(jnp.bfloat16)
+        far.append(
+            (go(far_out.at[d], passing.at[d], row[d]), go(far_stat, pass_stat.at[d], row[d]))
+        )
+    near = []
+    for d in range(2):
+        m, l = group(wrap(q + 1 - 2 * d), mixed)
+        pack(near_stat.at[d], m, l)
+        for copy in far[d]:
+            copy.wait_recv()
+        m_far = unpack(pass_stat.at[d], 0)
+        both = jnp.maximum(m, m_far)
+        joined = mixed[:, sides[d]] * jnp.exp(m - both) + passing[d].astype(jnp.float32) * jnp.exp(m_far - both)
+        near_out[d, :, sides[d]] = joined.astype(jnp.bfloat16)
+        near_out[d, :, sides[1 - d]] = mixed[:, sides[1 - d]].astype(jnp.bfloat16)
+        near.append(go(near_out.at[d], arriving.at[d], row[d]))
+        near.append(go(near_stat.at[d], arrive_stat.at[d], row[d]))
+        if d == 0:
+            near.append(go(pass_stat.at[0], arrive_far, row[0]))
+
+    m_own, l_own = group(q, own_mixed)
+    inner = scale * lax.dot_general(
+        q_buf[q], p_buf[...], (((1,), (1,)), ((), ())), preferred_element_type=jnp.float32
+    )
+    m_in = jnp.max(inner, axis=1, keepdims=True)
+    l_in = jnp.sum(jnp.exp(inner - m_in), axis=1, keepdims=True)
+    diagonal = lax.broadcasted_iota(jnp.int32, inner.shape, 0) == lax.broadcasted_iota(jnp.int32, inner.shape, 1)
+    positive = jnp.sum(jnp.where(diagonal, inner, 0.0), axis=1, keepdims=True)
+
+    for copy in near:
+        copy.wait_recv()
+    m_before, l_before = unpack(arrive_stat.at[0], 0), unpack(arrive_stat.at[0], 1)
+    m_after, l_after = unpack(arrive_stat.at[1], 0), unpack(arrive_stat.at[1], 1)
+    m_far, l_far = unpack(arrive_far, 0), unpack(arrive_far, 1)
+    m = m_in
+    for value in (m_own, m_before, m_after, m_far):
+        m = jnp.maximum(m, value)
+    total = l_in * jnp.exp(m_in - m)
+    for part_m, part_l in ((m_own, l_own), (m_before, l_before), (m_after, l_after), (m_far, l_far)):
+        total = total + part_l * jnp.exp(part_m - m)
+    losses = m + jnp.log(total) - positive
+    loss_ref[...] = jnp.broadcast_to(jnp.sum(losses, axis=0, keepdims=True), loss_ref.shape)
+    target = jnp.where(diagonal, 1.0, 0.0)
+    grad_full = (jnp.exp(inner - m) / total - target) * scale
+    grad_in = grad_full.astype(jnp.bfloat16)
+    by_own = jnp.exp(m_own - m) * (scale / total)
+    by_before = (
+        jnp.exp(jnp.maximum(m_before, m_far) - m) * (scale / total),
+        jnp.exp(m_before - m) * (scale / total),
+    )
+    by_after = (
+        jnp.exp(m_after - m) * (scale / total),
+        jnp.exp(jnp.maximum(m_after, m_far) - m) * (scale / total),
+    )
+    for n in range(width // 512):
+        part = pl.ds(n * 512, 512)
+        side = n * 512 // half
+        value = jnp.dot(grad_in, p_buf[:, part], preferred_element_type=jnp.float32)
+        value = value + own_mixed[:, part] * by_own
+        value = value + arriving[0, :, part].astype(jnp.float32) * by_before[side]
+        value = value + arriving[1, :, part].astype(jnp.float32) * by_after[side]
+        grad_ref[pl.ds(0, rows), part] = value.astype(jnp.bfloat16)
+    turned = grad_full.T.astype(jnp.bfloat16)
+    for n in range(width // 512):
+        part = pl.ds(n * 512, 512)
+        value = jnp.dot(turned, q_buf[q, :, part], preferred_element_type=jnp.float32)
+        grad_ref[pl.ds(rows, rows), part] = value.astype(jnp.bfloat16)
+    for copy in started:
+        copy.wait_send()
+
+
+def embedding_gradients(scale, all_q, blocks, emb_p, lists):
+    rows, width = emb_p.shape
+    count, block_rows = blocks.shape[0] * blocks.shape[1], blocks.shape[2]
+    blocks = blocks.reshape(count, block_rows, width)
+    places = lists.shape[1]
+    anywhere = pl.BlockSpec(memory_space=pl.ANY)
+    vmem = pl.BlockSpec(memory_space=pltpu.VMEM)
+    bf16, f32 = jnp.bfloat16, jnp.float32
+    return pl.pallas_call(
+        lambda *refs: partial_kernel(scale, *refs),
+        out_shape=(
+            jax.ShapeDtypeStruct((2 * rows, width), bf16),
+            jax.ShapeDtypeStruct((8, 128), f32),
+        ),
+        in_specs=[anywhere] * 3 + [pl.BlockSpec(memory_space=pltpu.SMEM), vmem],
+        out_specs=(vmem, vmem),
+        scratch_shapes=[
+            pltpu.VMEM(all_q.shape, bf16),
+            pltpu.VMEM(blocks.shape, bf16),
+            pltpu.VMEM((rows, width), bf16),
+            pltpu.VMEM((places * block_rows, width), bf16),
+            pltpu.VMEM((rows, places * block_rows), bf16),
+            pltpu.VMEM((rows, places * block_rows), f32),
+            pltpu.VMEM((rows, width), f32),
+            pltpu.VMEM((rows, width), f32),
+            pltpu.VMEM((2, rows, width // 2), bf16),
+            pltpu.VMEM((2, rows, width), bf16),
+            pltpu.VMEM((2, rows, width // 2), bf16),
+            pltpu.VMEM((2, rows, width), bf16),
+            pltpu.VMEM((8, 128), f32),
+            pltpu.VMEM((2, 8, 128), f32),
+            pltpu.VMEM((2, 8, 128), f32),
+            pltpu.VMEM((2, 8, 128), f32),
+            pltpu.VMEM((8, 128), f32),
+            pltpu.SemaphoreType.DMA((3,)),
+            pltpu.SemaphoreType.DMA((9,)),
+            pltpu.SemaphoreType.DMA((9,)),
+        ],
+        compiler_params=pltpu.CompilerParams(
+            collective_id=1, has_side_effects=True, vmem_limit_bytes=60 * 1024 * 1024
+        ),
+        name="embedding_gradients",
+    )(all_q, blocks, emb_p, lists, lists)
+
+
 def body(queries, passages, weight, bank, neg_ids, block_home):
     count_q = queries.shape[0]
-    slice_width = weight.shape[1]
+    features, slice_width = queries.shape[1], weight.shape[1]
     logit_scale = 1.0 / (SOFTMAX_TEMPER * math.sqrt(slice_width))
-    full_weight = lax.all_gather(weight, "fsdp", axis=0, tiled=True)
-    hidden = jnp.concatenate([queries, passages], axis=0)
-    embedded = jnp.dot(hidden, full_weight, preferred_element_type=jnp.float32).astype(jnp.bfloat16)
-    emb_q = embedded[:count_q]
-    emb_p = embedded[count_q:]
     n_dp = lax.axis_size("dp")
     n_fsdp = lax.axis_size("fsdp")
     per_dev = bank.shape[0]
-    block_rows = bank.shape[1]
     named = neg_ids.shape[1]
+    core = lax.rem(lax.axis_index("fsdp"), 2)
     slots = block_home[neg_ids[0]]
     owner = slots // per_dev // n_fsdp
     local = slots % per_dev
+    at_z, at_y = owner // RING, owner % RING
+    on_ring = jnp.where(core == 0, at_z, at_y)
+    on_row = jnp.where(core == 0, at_y, at_z)
     order = jnp.arange(named)
-    earlier = (owner[None, :] == owner[:, None]) & (order[None, :] < order[:, None])
+    earlier = (on_row[None, :] == on_row[:, None]) & (order[None, :] < order[:, None])
     rank = jnp.sum(earlier.astype(jnp.int32), axis=1)
-    peers = jnp.arange(n_dp)
-    places = jnp.arange(CAP)
-    hit = (owner[:, None, None] == peers[None, :, None]) & (
-        rank[:, None, None] == places[None, None, :]
+    hit = (on_row[:, None, None] == jnp.arange(RING)[None, :, None]) & (
+        rank[:, None, None] == jnp.arange(per_dev)[None, None, :]
     )
-    request = jnp.sum(jnp.where(hit, local[:, None, None] + 1, 0), axis=0) - 1
-    asked = lax.all_to_all(request, "dp", split_axis=0, concat_axis=0, tiled=True)
-    valid = asked >= 0
-    picked = jnp.take(bank, jnp.clip(asked, 0, per_dev - 1), axis=0)
-    picked = jnp.where(valid[:, :, None, None], picked, jnp.zeros_like(picked))
-    replies = lax.all_to_all(picked, "dp", split_axis=0, concat_axis=0, tiled=True)
-    replies = replies.reshape(n_dp * CAP, block_rows, slice_width)
-    negs = jnp.take(replies, owner * CAP + rank, axis=0).reshape(named * block_rows, slice_width)
-    inner = jnp.dot(emb_q, emb_p.T, preferred_element_type=jnp.float32) * logit_scale
-    outer = jnp.dot(emb_q, negs.T, preferred_element_type=jnp.float32) * logit_scale
-    scores = jnp.concatenate([inner, outer], axis=1)
-    top = jnp.max(scores, axis=1, keepdims=True)
-    expo = jnp.exp(scores - top)
-    total = jnp.sum(expo, axis=1, keepdims=True)
-    lse = top[:, 0] + jnp.log(total[:, 0])
-    loss_local = jnp.sum(lse - jnp.diagonal(inner))
-    target = jnp.concatenate(
-        [
-            jnp.eye(count_q, dtype=jnp.float32),
-            jnp.zeros((count_q, named * block_rows), jnp.float32),
-        ],
-        axis=1,
-    )
-    grad_s = ((expo / total - target) * logit_scale).astype(jnp.bfloat16)
-    grad_in = grad_s[:, :count_q]
-    grad_out = grad_s[:, count_q:]
-    query_gradient = (
-        jnp.dot(grad_in, emb_p, preferred_element_type=jnp.float32)
-        + jnp.dot(grad_out, negs, preferred_element_type=jnp.float32)
+    block = on_ring * per_dev + local
+    lists = jnp.sum(jnp.where(hit, block[:, None, None] + 1, 0), axis=0) - 1
+    lists = jnp.broadcast_to(lists[:, :, None], lists.shape + (128,))
+
+    blocks, all_q, emb_p, full_weight, all_lists = gather_and_embed(queries, passages, weight, bank, lists)
+    full_weight = full_weight.reshape(features, slice_width)
+    grad_rows, loss_local = embedding_gradients(logit_scale, all_q, blocks, emb_p, all_lists)
+    share = (
+        lax.dot_general(queries, grad_rows[:count_q], (((0,), (0,)), ((), ())), preferred_element_type=jnp.float32)
+        + lax.dot_general(passages, grad_rows[count_q:], (((0,), (0,)), ((), ())), preferred_element_type=jnp.float32)
     ).astype(jnp.bfloat16)
-    grad_p = lax.dot_general(
-        grad_in, emb_q, (((0,), (0,)), ((), ())), preferred_element_type=jnp.float32
-    ).astype(jnp.bfloat16)
-    grad_rows = jnp.concatenate([query_gradient, grad_p], axis=0)
-    back = lax.dot_general(
-        grad_rows, full_weight, (((1,), (1,)), ((), ())), preferred_element_type=jnp.float32
-    ).astype(jnp.bfloat16)
-    devices_all = n_dp * n_fsdp
-    share = lax.dot_general(
-        hidden, grad_rows, (((0,), (0,)), ((), ())), preferred_element_type=jnp.float32
-    ).astype(jnp.bfloat16)
-    grad_weight, losses = reduce_gradient(share, jnp.full((8, 128), loss_local, jnp.float32))
-    loss = losses[0, 0] / (count_q * devices_all)
-    return (loss, grad_weight, back[:count_q], back[count_q:])
+    grad_weight, losses = reduce_gradient(share, loss_local)
+    back = [
+        lax.dot_general(
+            grad_rows[i * count_q : (i + 1) * count_q],
+            full_weight,
+            (((1,), (1,)), ((), ())),
+            preferred_element_type=jnp.float32,
+        ).astype(jnp.bfloat16)
+        for i in range(2)
+    ]
+    loss = losses[0, 0] / (count_q * n_dp * n_fsdp)
+    return (loss, grad_weight, back[0], back[1])
 
 
 def solution(mesh):

time: 407 us -> 430 us (1.057)
  Pallas kernels: 42.6 us -> 384 us
  waiting for transfers between devices: 233 us -> 0 us
  local copies, waits for them, and re-layouts: 34.9 us -> 9.89 us
  other arithmetic: 25.6 us -> 1.06 us
  between operations: 16 us -> 2.53 us
  starting transfers between devices: 13.4 us -> 0 us
  matrix products: 41.1 us -> 31.6 us
    pallas_call x0 -> x2, Pallas kernels: none -> 343 us  [the longest x1 287 us: gather_and_embed(): pl.pallas_call(gather_kernel, out_shape=(jax.ShapeDtypeStruct((RING, many...]
    all_to_all x2 -> x0, waiting for transfers between devices: 219 us -> none  [the longest x1 212 us: body(): lax.all_to_all(picked, 'dp', split_axis=0, concat_axis=0, tiled=True)]
    gather x3 -> x0, local copies, waits for them, and re-layouts: 24.2 us -> none  [the longest x1 10.5 us: body(): jnp.take(replies, owner * CAP + rank, axis=0)]
    select_n x5 -> x1, other arithmetic: 21.9 us -> 0.03 us  [body(): on_row = jnp.where(core == 0, at_y, at_z)]
    all_to_all x2 -> x0, starting transfers between devices: 13.4 us -> none  [the longest x1 8.13 us: body(): lax.all_to_all(request, 'dp', split_axis=0, concat_axis=0, tiled=True)]
    all_gather x1 -> x0, waiting for transfers between devices: 12.9 us -> none  [body(): full_weight = lax.all_gather(weight, 'fsdp', axis=0, tiled=True)]
    dot_general x8 -> x4, matrix products: 41.1 us -> 31.6 us  [the longest x2 13.1 us: body(): lax.dot_general(grad_rows[i * count_q:(i + 1) * count_q], full_weight, ((...]
    unnamed x20 -> x27, local copies, waits for them, and re-layouts: 4.25 us -> 8.66 us
  transfers between devices with their start and end apart: 3 -> 0, of which waited for: 3 -> 0; matrix products, arithmetic and copies ran while one was open for 10% -> 0% of each run, Pallas kernels for 0% -> 0%
where the time goes in v2:
time: 430 us; the launch traced here: 429 us
  Pallas kernels  384 us (89%)
  matrix products  31.6 us (7%)
  local copies, waits for them, and re-layouts  9.89 us (2%)
    pallas_call x1, Pallas kernels, gather_and_embed(): pl.pallas_call(gather_kernel, out_shape=(jax.ShapeDtypeStruct((RING, many...  287 us
    pallas_call x1, Pallas kernels, embedding_gradients(): pl.pallas_call(lambda *refs: partial_kernel(scale, *refs), out_shape=(jax...  56.3 us
    pallas_call x1, Pallas kernels, reduce_gradient(): pl.pallas_call(reduce_kernel, out_shape=(jax.ShapeDtypeStruct((ROWS, widt...  40.9 us
    dot_general x2, matrix products, body(): lax.dot_general(grad_rows[i * count_q:(i + 1) * count_q], full_weight, ((...  13.1 us
    dot_general x1, matrix products, body(): lax.dot_general(passages, grad_rows[count_q:], (((0,), (0,)), ((), ())),...  10.3 us
    unnamed x27, local copies, waits for them, and re-layouts  8.66 us

profile of v2, /device:TPU:0, one launch (start us, length us, event | category | flops | bytes accessed | tf_op | source)
XLA Modules:
  0.0 429.3 jit_solution(5780820371451629457)
XLA Ops:
  0.6 0.0 copy-start
  0.7 0.7 fusion.8
  1.3 0.0 copy-done
  1.3 0.6 gather_fusion
  2.0 0.2 convert_reduce_fusion
  2.2 0.1 select_reduce_fusion
  2.4 0.1 broadcast_in_dim.12.list_ref
  2.5 1.4 copy-done.2
  3.9 1.4 copy-done.4
  5.3 2.2 copy-done.6
  7.5 1.2 copy-done.8
  8.7 287.0 %gather_and_embed.1 = (bf16[4,8,128,2048]{3,2,1,0:T(8,128)(2,1)}, bf16[4,384,2048]{2,1,0:T(8,128)(2,1)}, bf16[384,2048]{1,0:T(8,128)(2,1)S(1)}, bf16[8,256,2048]{2,1,0:T(8,128)(2,1)}, s32[4,8,128]{2,1,0:T(8,128)S(1)}) custom-call(bf16[384,2048]{1,0:T(8,128)(2,1)S(1)} %copy-done.4, bf16[384,2048]{1,0:T(8,128)(2,1)S(1)} %copy-done.2, ...), custom_call_target="tpu_custom_call" | custom-call | tf_op jit(solution)/shard_map/gather_and_embed/pallas_call | solution.py:429
  295.7 0.0 copy-start.7
  295.7 1.1 copy-done.7
  296.9 0.6 copy-done.9
  297.5 56.3 %embedding_gradients.1 = (bf16[768,2048]{1,0:T(8,128)(2,1)}, f32[8,128]{1,0:T(8,128)}) custom-call(bf16[4,384,2048]{2,1,0:T(8,128)(2,1)} %get-tuple-element.13.refs_0_, bf16[32,128,2048]{2,1,0:T(8,128)(2,1)} %bitcast.15, bf16[384,2048]{1,0:T(8,128)(2,1)} %copy-done.7, s32[4,8,128]{2,1,0:T(8,128)} %copy-done.9, s32[4,8,128]{2,1,0:T(8,128)} %copy-done.9), custom_call_target="tpu_custom_call" | custom-call | tf_op jit(solution)/shard_map/embedding_gradients/pallas_call | solution.py:629
  353.8 0.0 copy-start.11
  353.8 8.6 %convolution_convert_fusion.1 = bf16[384,2048]{1,0:T(8,128)(2,1)} fusion(bf16[2048,2048]{1,0:T(8,128)(2,1)} %bitcast.16, bf16[768,2048]{1,0:T(8,128)(2,1)} %get-tuple-element.17), kind=kOutput, calls=%fused_computation.3 | convolution fusion | flops 3222011904 | bytes 11534336 | tf_op jit(solution)/shard_map/dot_general | solution.py:700
  362.4 4.6 %convolution_convert_fusion = bf16[384,2048]{1,0:T(8,128)(2,1)} fusion(bf16[2048,2048]{1,0:T(8,128)(2,1)S(1)} %bitcast.17, bf16[768,2048]{1,0:T(8,128)(2,1)S(1)} %copy-done.11), kind=kOutput, calls=%fused_computation.2 | convolution fusion | flops 3222011904 | bytes 11534336 | tf_op jit(solution)/shard_map/dot_general | solution.py:700
  367.0 8.2 %fusion.3 = f32[2048,2048]{0,1:T(8,128)} fusion(bf16[384,2048]{1,0:T(8,128)(2,1)S(1)} %copy-done.5, bf16[768,2048]{1,0:T(8,128)(2,1)S(1)} %copy-done.11), kind=kOutput, calls=%fused_computation.7 | convolution fusion | flops 3221225472 | bytes 19922944 | tf_op jit(solution)/shard_map/dot_general | solution.py:695
  375.2 10.3 %add_convert_fusion = bf16[2048,2048]{0,1:T(8,128)(2,1)} fusion(f32[2048,2048]{0,1:T(8,128)} %fusion.3, bf16[384,2048]{1,0:T(8,128)(2,1)S(1)} %copy-done.3, bf16[768,2048]{1,0:T(8,128)(2,1)S(1)} %copy-done.11), kind=kOutput, calls=%fused_computation.1 | convolution fusion | flops 3229614080 | bytes 28311552 | tf_op jit(solution)/shard_map/dot_general | solution.py:696
  385.4 40.9 %reduce_gradient.1 = (f32[16,2048]{1,0:T(8,128)S(1)}, f32[8,128]{1,0:T(8,128)S(1)}) custom-call(bf16[4,4,4,2,16,2048]{5,4,3,2,1,0:T(8,128)(2,1)} %bitcast.14, f32[8,128]{1,0:T(8,128)S(1)} %copy-done.10), custom_call_target="tpu_custom_call" | custom-call | tf_op jit(solution)/shard_map/reduce_gradient/pallas_call | solution.py:254
  426.4 0.5 slice.13
  427.5 0.7 copy.11
  (22 shorter events, 0.1 us)
Async XLA Ops:
  0.6 0.7 copy-start
  2.5 1.4 copy-start.2
  3.9 1.4 copy-start.4
  5.3 2.2 copy-start.6
  7.5 1.2 copy-start.8
  295.7 1.1 copy-start.7
  296.9 0.6 copy-start.9
  353.8 8.6 %copy-start.11 = (bf16[768,2048]{1,0:T(8,128)(2,1)S(1)}, bf16[768,2048]{1,0:T(8,128)(2,1)}, u32[]{:S(2)}) copy-start(bf16[768,2048]{1,0:T(8,128)(2,1)} %get-tuple-element.17) | copy-start | bytes 9437188
  353.8 8.6 %copy-start.12 = (bf16[8,256,2048]{2,1,0:T(8,128)(2,1)S(1)}, bf16[8,256,2048]{2,1,0:T(8,128)(2,1)}, u32[]{:S(2)}) copy-start(bf16[8,256,2048]{2,1,0:T(8,128)(2,1)} %get-tuple-element.21) | copy-start | bytes 25165828
  362.4 4.6 %copy-start.5 = (bf16[384,2048]{1,0:T(8,128)(2,1)S(1)}, bf16[384,2048]{1,0:T(8,128)(2,1)}, u32[]{:S(2)}) copy-start(bf16[384,2048]{1,0:T(8,128)(2,1)} %q_ref.1) | copy-start | bytes 4718596
  367.0 8.2 %copy-start.3 = (bf16[384,2048]{1,0:T(8,128)(2,1)S(1)}, bf16[384,2048]{1,0:T(8,128)(2,1)}, u32[]{:S(2)}) copy-start(bf16[384,2048]{1,0:T(8,128)(2,1)} %p_ref.1) | copy-start | bytes 4718596
  375.1 10.3 %copy-start.10 = (f32[8,128]{1,0:T(8,128)S(1)}, f32[8,128]{1,0:T(8,128)}, u32[]{:S(2)}) copy-start(f32[8,128]{1,0:T(8,128)} %get-tuple-element.18.loss_ref) | copy-start | bytes 12292
  385.4 42.8 %copy-start.1 = (s32[1024]{0:T(1024)S(1)}, s32[1024]{0:T(1024)}, u32[]{:S(2)}) copy-start(s32[1024]{0:T(1024)} %param.11) | copy-start | bytes 12292

commit v3 on v2

--- a/solution.py
+++ b/solution.py
@@ -11,6 +11,7 @@
 
 MESH = pl.DeviceIdType.MESH
 RING = 4
+BACK = ((0, 2), (2, 4), (4, 5), (5, 6), (6, 7), (7, 8))
 ROWS = 16
 PARTS = (
     (0, 768, 384, (2, 1, 0)),
@@ -52,17 +53,41 @@
     return tuple(index if i == spot else slice(None) for i in range(rank)) + (slice(None), columns)
 
 
-def reduce_kernel(share_ref, loss_ref, out_ref, total_ref, *scratch):
+def reduce_kernel(turned_ref, grad_ref, w_ref, loss_ref, out_ref, total_ref, backq_ref, backp_ref, *scratch):
     coords, core = position()
     sibling = device(coords, 1 - core)
     near = [[device(shifted(coords, a, by), core) for by in (1, 3)] for a in range(3)]
     far = [device(shifted(coords, a, 2), core) for a in range(3)]
+    t_buf, w_buf, local_sem = scratch[-3:]
+    scratch = scratch[:-3]
+    take = [
+        pltpu.make_async_copy(turned_ref, t_buf, local_sem.at[0]),
+        pltpu.make_async_copy(w_ref, w_buf, local_sem.at[1]),
+    ]
+    for copy in take:
+        copy.start()
     greet([sibling] + [d for pair in near for d in pair] + far)
+    rows = backq_ref.shape[0]
+
+    def back(lo, hi):
+        @pl.loop(lo, hi)
+        def _(n):
+            value = lax.dot_general(
+                grad_ref[...], w_buf[n], (((1,), (1,)), ((), ())), preferred_element_type=jnp.float32
+            ).astype(jnp.bfloat16)
+            columns = pl.ds(pl.multiple_of(n * w_buf.shape[1], 256), w_buf.shape[1])
+            backq_ref[:, columns] = value[:rows]
+            backp_ref[:, columns] = value[rows:]
+
+    def share(which, i, columns):
+        chunk = t_buf[which, pl.ds(pl.multiple_of(i * 256, 256), 256)]
+        value = jnp.dot(chunk, grad_ref[:, columns], preferred_element_type=jnp.float32)
+        return value.reshape((RING, RING, ROWS) + value.shape[1:])
 
     count = len(PARTS)
-    paired = scratch[0]
-    sums = [[scratch[1 + 3 * p + k] for k in range(3)] for p in range(count)]
-    base = 1 + 3 * count
+    paired, outgoing = scratch[:count], scratch[count : 2 * count]
+    sums = [[scratch[2 * count + 3 * p + k] for k in range(3)] for p in range(count)]
+    base = 5 * count
     passing = [[[scratch[base + 6 * p + 2 * k + d] for d in range(2)] for k in range(3)] for p in range(count)]
     base += 6 * count
     arriving = [[scratch[base + 3 * p + k] for k in range(3)] for p in range(count)]
@@ -76,20 +101,16 @@
         started.append(copy)
         return copy
 
+    take[0].wait()
     first = []
     for p, (lo, width, cut, order) in enumerate(PARTS):
         columns = pl.ds(lo, width)
-        first.append(
-            go(
-                remote(
-                    share_ref.at[:, :, :, 1 - core, :, columns],
-                    paired.at[:, :, :, :, columns],
-                    send0.at[p],
-                    recv0.at[p],
-                    sibling,
-                )
-            )
-        )
+
+        @pl.loop(0, RING)
+        def _(i):
+            outgoing[p][i] = share(1 - core, i, columns).astype(jnp.bfloat16)
+
+        first.append(go(remote(outgoing[p], paired[p], send0.at[p], recv0.at[p], sibling)))
 
     loss_buf[0, pl.ds(core, 1)] = loss_ref[...][None]
     pair_loss = go(
@@ -208,17 +229,20 @@
 
         @pl.loop(0, RING)
         def _(i):
-            a = share_ref[i, :, :, core, :, columns].astype(jnp.float32)
-            b = paired[i, :, :, :, columns].astype(jnp.float32)
-            sums[p][0][i] = (a + b).astype(jnp.bfloat16)
+            value = share(core, i, columns) + paired[p][i].astype(jnp.float32)
+            sums[p][0][i] = value.astype(jnp.bfloat16)
 
         moves.append(begin(p, 0))
 
     value = loss_step(0, [pair_loss], 2)
     for k in range(3):
         loss_copies = loss_send_axis(1 + k, k, value)
+        if k == 0:
+            take[1].wait()
+        back(*BACK[2 * k])
         for p in range(count):
             relay(p, k, moves[p])
+        back(*BACK[2 * k + 1])
         for p in range(count):
             finish(p, k, moves[p])
             if k < 2:
@@ -229,10 +253,11 @@
         copy.wait_send()
 
 
-def reduce_gradient(share, loss):
-    width = share.shape[1]
-    share = share.reshape(RING, RING, RING, 2, ROWS, width)
-    scratch = [pltpu.VMEM((RING, RING, RING, ROWS, width), jnp.bfloat16)]
+def reduce_gradient(turned, grad_rows, full_weight, loss):
+    width = grad_rows.shape[1]
+    rows = grad_rows.shape[0] // 2
+    features = full_weight.shape[0] * full_weight.shape[1]
+    scratch = [pltpu.VMEM((RING,) * 3 + (ROWS, columns), jnp.bfloat16) for _, columns, _, _ in PARTS] * 2
     for _, columns, _, _ in PARTS:
         scratch += [pltpu.VMEM((RING,) * (3 - k) + (ROWS, columns), jnp.bfloat16) for k in range(3)]
     for _, columns, cut, _ in PARTS:
@@ -249,22 +274,28 @@
         pltpu.SemaphoreType.DMA((len(PARTS), 3, 6)),
         pltpu.SemaphoreType.DMA((4, 3)),
         pltpu.SemaphoreType.DMA((4, 3)),
+        pltpu.VMEM(turned.shape, jnp.bfloat16),
+        pltpu.VMEM(full_weight.shape, jnp.bfloat16),
+        pltpu.SemaphoreType.DMA((2,)),
     ]
+    hbm = pl.BlockSpec(memory_space=pltpu.HBM)
     vmem = pl.BlockSpec(memory_space=pltpu.VMEM)
     return pl.pallas_call(
         reduce_kernel,
         out_shape=(
             jax.ShapeDtypeStruct((ROWS, width), jnp.float32),
             jax.ShapeDtypeStruct((8, 128), jnp.float32),
+            jax.ShapeDtypeStruct((rows, features), jnp.bfloat16),
+            jax.ShapeDtypeStruct((rows, features), jnp.bfloat16),
         ),
-        in_specs=[vmem, vmem],
-        out_specs=(vmem, vmem),
+        in_specs=[hbm, vmem, hbm, vmem],
+        out_specs=(vmem,) * 4,
         scratch_shapes=scratch,
         compiler_params=pltpu.CompilerParams(
             collective_id=2, has_side_effects=True, vmem_limit_bytes=48 * 1024 * 1024
         ),
         name="reduce_gradient",
-    )(share, loss)
+    )(turned, grad_rows, full_weight, loss)
 
 
 def ring_position():
@@ -283,11 +314,11 @@
 
 def gather_kernel(
     q_ref, p_ref, w_ref, bank_ref, list_ref,
-    blocks_ref, allq_ref, embp_ref, full_ref, lists_ref,
-    w_buf, h_buf, acc, embq, embp, list_buf, local_sem, send, recv,
+    blocks_ref, allq_ref, embp_ref, full_ref, turned_ref, lists_ref,
+    w_buf, h_buf, t_buf, acc, embq, embp, list_buf, local_sem, send, recv,
 ):
     r, q, x, core = ring_position()
-    sibling = ring_device(r, q, x, 1 - core)
+    sibling = ring_device(q, r, x, 1 - core)
     ring = [ring_device(r + by, q, x, core) for by in (1, -1)]
     row = [ring_device(r, q + by, x, core) for by in (1, -1)]
     row_far = ring_device(r, q + 2, x, core)
@@ -361,6 +392,15 @@
     w_pair.wait_recv()
     multiply(other)
 
+    @pl.loop(0, h_buf.shape[1] // 256)
+    def _(n):
+        tile = h_buf[:, pl.ds(pl.multiple_of(n * 256, 256), 256)].T
+        for i in range(256 // ROWS):
+            place = pl.ds(pl.multiple_of(n * 128 + i // 2 * ROWS, ROWS), ROWS)
+            t_buf[i % 2, place] = tile[i * ROWS : (i + 1) * ROWS]
+
+    keep_t = keep(t_buf, turned_ref)
+
     across = []
     w_far = [None, None]
     for n in range(2):
@@ -424,7 +464,7 @@
     depth, width = weight.shape
     parts = features // depth
     many, block_rows = bank.shape[:2]
-    anywhere = pl.BlockSpec(memory_space=pl.ANY)
+    anywhere = pl.BlockSpec(memory_space=pltpu.HBM)
     vmem = pl.BlockSpec(memory_space=pltpu.VMEM)
     return pl.pallas_call(
         gather_kernel,
@@ -433,18 +473,20 @@
             jax.ShapeDtypeStruct((RING, rows, width), jnp.bfloat16),
             jax.ShapeDtypeStruct((rows, width), jnp.bfloat16),
             jax.ShapeDtypeStruct((parts, depth, width), jnp.bfloat16),
+            jax.ShapeDtypeStruct((2, features // 2, 2 * rows), jnp.bfloat16),
             jax.ShapeDtypeStruct(lists.shape, jnp.int32),
         ),
         in_specs=[anywhere] * 4 + [vmem],
-        out_specs=(anywhere,) * 4 + (vmem,),
+        out_specs=(anywhere,) * 5 + (vmem,),
         scratch_shapes=[
             pltpu.VMEM((parts, depth, width), jnp.bfloat16),
             pltpu.VMEM((2 * rows, features), jnp.bfloat16),
+            pltpu.VMEM((2, features // 2, 2 * rows), jnp.bfloat16),
             pltpu.VMEM((2 * rows, width), jnp.float32),
             pltpu.VMEM((rows, width), jnp.bfloat16),
             pltpu.VMEM((rows, width), jnp.bfloat16),
             pltpu.VMEM(lists.shape, jnp.int32),
-            pltpu.SemaphoreType.DMA((7,)),
+            pltpu.SemaphoreType.DMA((8,)),
             pltpu.SemaphoreType.DMA((28,)),
             pltpu.SemaphoreType.DMA((28,)),
         ],
@@ -623,7 +665,7 @@
     count, block_rows = blocks.shape[0] * blocks.shape[1], blocks.shape[2]
     blocks = blocks.reshape(count, block_rows, width)
     places = lists.shape[1]
-    anywhere = pl.BlockSpec(memory_space=pl.ANY)
+    anywhere = pl.BlockSpec(memory_space=pltpu.HBM)
     vmem = pl.BlockSpec(memory_space=pltpu.VMEM)
     bf16, f32 = jnp.bfloat16, jnp.float32
     return pl.pallas_call(
@@ -665,7 +707,7 @@
 
 def body(queries, passages, weight, bank, neg_ids, block_home):
     count_q = queries.shape[0]
-    features, slice_width = queries.shape[1], weight.shape[1]
+    slice_width = weight.shape[1]
     logit_scale = 1.0 / (SOFTMAX_TEMPER * math.sqrt(slice_width))
     n_dp = lax.axis_size("dp")
     n_fsdp = lax.axis_size("fsdp")
@@ -688,25 +730,11 @@
     lists = jnp.sum(jnp.where(hit, block[:, None, None] + 1, 0), axis=0) - 1
     lists = jnp.broadcast_to(lists[:, :, None], lists.shape + (128,))
 
-    blocks, all_q, emb_p, full_weight, all_lists = gather_and_embed(queries, passages, weight, bank, lists)
-    full_weight = full_weight.reshape(features, slice_width)
+    blocks, all_q, emb_p, full_weight, turned, all_lists = gather_and_embed(queries, passages, weight, bank, lists)
     grad_rows, loss_local = embedding_gradients(logit_scale, all_q, blocks, emb_p, all_lists)
-    share = (
-        lax.dot_general(queries, grad_rows[:count_q], (((0,), (0,)), ((), ())), preferred_element_type=jnp.float32)
-        + lax.dot_general(passages, grad_rows[count_q:], (((0,), (0,)), ((), ())), preferred_element_type=jnp.float32)
-    ).astype(jnp.bfloat16)
-    grad_weight, losses = reduce_gradient(share, loss_local)
-    back = [
-        lax.dot_general(
-            grad_rows[i * count_q : (i + 1) * count_q],
-            full_weight,
-            (((1,), (1,)), ((), ())),
-            preferred_element_type=jnp.float32,
-        ).astype(jnp.bfloat16)
-        for i in range(2)
-    ]
+    grad_weight, losses, back_q, back_p = reduce_gradient(turned, grad_rows, full_weight, loss_local)
     loss = losses[0, 0] / (count_q * n_dp * n_fsdp)
-    return (loss, grad_weight, back[0], back[1])
+    return (loss, grad_weight, back_q, back_p)
 
 
 def solution(mesh):

time: 430 us -> 223 us (0.52)
  Pallas kernels: 384 us -> 204 us
  matrix products: 31.6 us -> 0 us
  local copies, waits for them, and re-layouts: 9.89 us -> 14.4 us
    pallas_call x1, Pallas kernels: 287 us -> 103 us  [gather_and_embed(): pl.pallas_call(gather_kernel, out_shape=(jax.ShapeDtypeStruct((RING, many...]
    dot_general x4 -> x0, matrix products: 31.6 us -> none  [the longest x2 13.1 us: body(): lax.dot_general(grad_rows[i * count_q:(i + 1) * count_q], full_weight, ((...]
    unnamed x27 -> x21, local copies, waits for them, and re-layouts: 8.66 us -> 13.2 us
    pallas_call x1, Pallas kernels: 40.9 us -> 45.4 us  [reduce_gradient(): pl.pallas_call(reduce_kernel, out_shape=(jax.ShapeDtypeStruct((ROWS, widt...]
where the time goes in v3:
time: 223 us; the launch traced here: 222 us
  Pallas kernels  204 us (91%)
  local copies, waits for them, and re-layouts  14.4 us (6%)
  between operations  2.51 us (1%)
    pallas_call x1, Pallas kernels, gather_and_embed(): pl.pallas_call(gather_kernel, out_shape=(jax.ShapeDtypeStruct((RING, many...  103 us
    pallas_call x1, Pallas kernels, embedding_gradients(): pl.pallas_call(lambda *refs: partial_kernel(scale, *refs), out_shape=(jax...  56.4 us
    pallas_call x1, Pallas kernels, reduce_gradient(): pl.pallas_call(reduce_kernel, out_shape=(jax.ShapeDtypeStruct((ROWS, widt...  45.4 us
    unnamed x21, local copies, waits for them, and re-layouts  13.2 us

profile of v3, /device:TPU:0, one launch (start us, length us, event | category | flops | bytes accessed | tf_op | source)
XLA Modules:
  0.0 222.4 jit_solution(8579869266123440173)
XLA Ops:
  0.6 0.0 copy-start
  0.7 0.7 fusion.3
  1.3 0.0 copy-done
  1.3 0.6 gather_fusion
  2.0 0.2 convert_reduce_fusion
  2.2 0.1 select_reduce_fusion
  2.4 0.1 broadcast_in_dim.12.list_ref
  2.5 2.2 copy-done.1
  4.7 1.4 copy-done.3
  6.1 1.4 copy-done.4
  7.5 1.2 copy-done.6
  8.7 102.6 %gather_and_embed.1 = (bf16[4,8,128,2048]{3,2,1,0:T(8,128)(2,1)}, bf16[4,384,2048]{2,1,0:T(8,128)(2,1)}, bf16[384,2048]{1,0:T(8,128)(2,1)S(1)}, bf16[8,256,2048]...) custom-call(bf16[384,2048]{1,0:T(8,128)(2,1)S(1)} %copy-done.3, ...), custom_call_target="tpu_custom_call" | custom-call | tf_op jit(solution)/shard_map/gather_and_embed/pallas_call | solution.py:469
  111.3 0.0 copy-start.2
  111.3 1.6 copy-done.2
  112.9 1.1 copy-done.5
  114.0 0.6 copy-done.7
  114.6 56.4 %embedding_gradients.1 = (bf16[768,2048]{1,0:T(8,128)(2,1)}, f32[8,128]{1,0:T(8,128)}) custom-call(bf16[4,384,2048]{2,1,0:T(8,128)(2,1)} %get-tuple-element.17.refs_0_, bf16[32,128,2048]{2,1,0:T(8,128)(2,1)} %bitcast.6, bf16[384,2048]{1,0:T(8,128)(2,1)} %copy-done.5, s32[4,8,128]{2,1,0:T(8,128)} %copy-done.7, s32[4,8,128]{2,1,0:T(8,128)} %copy-done.7), custom_call_target="tpu_custom_call" | custom-call | tf_op jit(solution)/shard_map/embedding_gradients/pallas_call | solution.py:671
  171.0 0.0 copy-start.8
  171.1 0.7 copy-done.8
  171.7 45.4 %reduce_gradient.1 = (f32[16,2048]{1,0:T(8,128)S(1)}, f32[8,128]{1,0:T(8,128)S(1)}, bf16[384,2048]{1,0:T(8,128)(2,1)S(1)}, bf16[384,2048]{1,0:T(8,128)(2,1)S(1)}) custom-call(bf16[2,1024,768]{2,1,0:T(8,128)(2,1)} %copy-done.2, bf16[768,2048]{1,0:T(8,128)(2,1)} %get-tuple-element.21.grad_ref, bf16[8,256,2048]{2,1,0:T(8,128)(2,1)} %get-tuple-element.22.w_ref, ...), custom_call_target="tpu_custom_call" | custom-call | tf_op jit(solution)/shard_map/reduce_gradient/pallas_call | solution.py:283
  217.2 0.5 slice.3
  218.3 0.7 copy.13
  219.0 1.1 copy.14
  220.1 1.1 copy.15
  (12 shorter events, 0.1 us)
Async XLA Ops:
  0.6 0.7 copy-start
  2.5 2.2 copy-start.1
  4.6 1.4 copy-start.3
  6.1 1.4 copy-start.4
  7.5 1.2 copy-start.6
  111.3 1.6 copy-start.2
  112.9 1.1 copy-start.5
  114.0 0.6 copy-start.7
  171.0 0.7 copy-start.8

commit v4 on v3

--- a/solution.py
+++ b/solution.py
@@ -10,6 +10,8 @@
 SOFTMAX_TEMPER = 0.25
 
 MESH = pl.DeviceIdType.MESH
+VMEM_LIMIT = 63 * 1024 * 1024
+TILE = 512
 RING = 4
 BACK = ((0, 2), (2, 4), (4, 5), (5, 6), (6, 7), (7, 8))
 ROWS = 16
@@ -53,16 +55,17 @@
     return tuple(index if i == spot else slice(None) for i in range(rank)) + (slice(None), columns)
 
 
-def reduce_kernel(turned_ref, grad_ref, w_ref, loss_ref, out_ref, total_ref, backq_ref, backp_ref, *scratch):
+def reduce_kernel(turned_ref, rows_ref, w_ref, loss_ref, out_ref, total_ref, backq_ref, backp_ref, *scratch):
     coords, core = position()
     sibling = device(coords, 1 - core)
     near = [[device(shifted(coords, a, by), core) for by in (1, 3)] for a in range(3)]
     far = [device(shifted(coords, a, 2), core) for a in range(3)]
-    t_buf, w_buf, local_sem = scratch[-3:]
-    scratch = scratch[:-3]
+    t_buf, grad_ref, w_buf, local_sem = scratch[-4:]
+    scratch = scratch[:-4]
     take = [
         pltpu.make_async_copy(turned_ref, t_buf, local_sem.at[0]),
-        pltpu.make_async_copy(w_ref, w_buf, local_sem.at[1]),
+        pltpu.make_async_copy(rows_ref, grad_ref, local_sem.at[1]),
+        pltpu.make_async_copy(w_ref, w_buf, local_sem.at[2]),
     ]
     for copy in take:
         copy.start()
@@ -102,6 +105,7 @@
         return copy
 
     take[0].wait()
+    take[1].wait()
     first = []
     for p, (lo, width, cut, order) in enumerate(PARTS):
         columns = pl.ds(lo, width)
@@ -238,7 +242,7 @@
     for k in range(3):
         loss_copies = loss_send_axis(1 + k, k, value)
         if k == 0:
-            take[1].wait()
+            take[2].wait()
         back(*BACK[2 * k])
         for p in range(count):
             relay(p, k, moves[p])
@@ -275,8 +279,9 @@
         pltpu.SemaphoreType.DMA((4, 3)),
         pltpu.SemaphoreType.DMA((4, 3)),
         pltpu.VMEM(turned.shape, jnp.bfloat16),
+        pltpu.VMEM(grad_rows.shape, jnp.bfloat16),
         pltpu.VMEM(full_weight.shape, jnp.bfloat16),
-        pltpu.SemaphoreType.DMA((2,)),
+        pltpu.SemaphoreType.DMA((3,)),
     ]
     hbm = pl.BlockSpec(memory_space=pltpu.HBM)
     vmem = pl.BlockSpec(memory_space=pltpu.VMEM)
@@ -288,7 +293,7 @@
             jax.ShapeDtypeStruct((rows, features), jnp.bfloat16),
             jax.ShapeDtypeStruct((rows, features), jnp.bfloat16),
         ),
-        in_specs=[hbm, vmem, hbm, vmem],
+        in_specs=[hbm, hbm, hbm, vmem],
         out_specs=(vmem,) * 4,
         scratch_shapes=scratch,
         compiler_params=pltpu.CompilerParams(
@@ -312,10 +317,16 @@
     return (r * (RING - (RING - 1) * core) + q * (1 + (RING - 1) * core), x * 2 + core)
 
 
-def gather_kernel(
-    q_ref, p_ref, w_ref, bank_ref, list_ref,
-    blocks_ref, allq_ref, embp_ref, full_ref, turned_ref, lists_ref,
-    w_buf, h_buf, t_buf, acc, embq, embp, list_buf, local_sem, send, recv,
+NONE = -1e30
+
+
+def embed_kernel(
+    scale, q_ref, p_ref, w_ref, bank_ref, list_ref,
+    full_ref, turned_ref, grad_ref, loss_ref,
+    w_buf, h_buf, t_buf, acc, q_buf, x_buf, p_buf, prob, score, inner,
+    far_out, near_out, passing, arriving,
+    far_stat, near_stat, pass_stat, arrive_stat, arrive_far,
+    list_buf, index_buf, local_sem, send, recv,
 ):
     r, q, x, core = ring_position()
     sibling = ring_device(q, r, x, 1 - core)
@@ -323,9 +334,11 @@
     row = [ring_device(r, q + by, x, core) for by in (1, -1)]
     row_far = ring_device(r, q + 2, x, core)
     line = [ring_device(r, q, x + by, core) for by in (1, -1)]
-    rows = q_ref.shape[0]
+    rows, width = p_buf.shape
     depth = w_ref.shape[0]
     many = bank_ref.shape[0]
+    places = list_ref.shape[1]
+    half = width // 2
     own = x * 2 + core
     other = x * 2 + 1 - core
 
@@ -355,8 +368,10 @@
     greet([sibling] + ring + row + [row_far] + line)
 
     cut_w = (pl.ds(0, depth // 2), pl.ds(depth // 2, depth // 2))
-    cut_b = (pl.ds(0, many // 2), pl.ds(many // 2, many // 2))
     cut_q = (pl.ds(0, rows // 2), pl.ds(rows // 2, rows // 2))
+
+    def blocks(home, h):
+        return x_buf.at[pl.ds(home * many + h * (many // 2), many // 2)]
 
     w_pair = go(w_ref, w_buf.at[own], sibling)
     w_near = [None, None]
@@ -364,26 +379,28 @@
     for d in range(2):
         w_near[d] = [go(w_ref.at[cut_w[h]], w_buf.at[own, cut_w[h]], line[d]) for h in (d, 1 - d)]
     for d in range(2):
-        b_near[d] = [go(bank_ref.at[cut_b[h]], blocks_ref.at[r, cut_b[h]], ring[d]) for h in (d, 1 - d)]
+        b_near[d] = [
+            go(bank_ref.at[pl.ds(h * (many // 2), many // 2)], blocks(r, h), ring[d]) for h in (d, 1 - d)
+        ]
     list_copies = [
         go(list_ref.at[wrap(q + by)], list_buf.at[q], target) for by, target in ((1, row[0]), (-1, row[1]), (2, row_far))
     ]
     list_buf[pl.ds(q, 1)] = list_ref[pl.ds(q, 1)]
-    keep_b = keep(bank_ref, blocks_ref.at[r])
+    take_b = keep(bank_ref, x_buf.at[pl.ds(r * many, many)])
 
     def multiply(part, first=False):
-        @pl.loop(0, acc.shape[1] // 512)
+        @pl.loop(0, width // 512)
         def _(n):
             columns = pl.ds(pl.multiple_of(n * 512, 512), 512)
             term = jnp.dot(
                 h_buf[:, pl.ds(pl.multiple_of(part * depth, depth), depth)],
                 w_buf[part, :, columns],
                 preferred_element_type=jnp.float32,
-            )
+            ).reshape(2, rows, 512)
             if first:
-                acc[:, columns] = term
+                acc[:, :, columns] = term
             else:
-                acc[:, columns] += term
+                acc[:, :, columns] += term
 
     take_q.wait()
     take_p.wait()
@@ -403,6 +420,7 @@
 
     across = []
     w_far = [None, None]
+    w_sent = []
     for n in range(2):
         for d in range(2):
             h = d if n == 0 else 1 - d
@@ -411,13 +429,14 @@
             if n == 0:
                 w_far[d] = go(w_buf.at[came, cut_w[h]], w_buf.at[came, cut_w[h]], line[d])
             across.append(go(w_buf.at[came, cut_w[h]], w_buf.at[came, cut_w[h]], sibling))
+    w_sent += w_far + across
     multiply(wrap(x - 1) * 2 + core)
     multiply(wrap(x + 1) * 2 + core)
     b_far = [None, None]
     for d in range(2):
         came = wrap(r - 1 + 2 * d)
         b_near[d][0].wait_recv()
-        b_far[d] = go(blocks_ref.at[came, cut_b[d]], blocks_ref.at[came, cut_b[d]], ring[d])
+        b_far[d] = go(blocks(came, d), blocks(came, d), ring[d])
     for copy in across:
         copy.wait_recv()
     multiply(wrap(x - 1) * 2 + 1 - core)
@@ -427,115 +446,37 @@
     for d in range(2):
         w_far[d].wait_recv()
         across.append(go(w_buf.at[last + core, cut_w[d]], w_buf.at[last + core, cut_w[d]], sibling))
+    w_sent += across
     multiply(last + core)
     for copy in across:
         copy.wait_recv()
     multiply(last + 1 - core)
 
-    embq[...] = acc[pl.ds(0, rows)].astype(jnp.bfloat16)
+    q_buf[pl.ds(q, 1)] = acc[pl.ds(0, 1)].astype(jnp.bfloat16)
     q_near = [None, None]
     for d in range(2):
-        q_near[d] = [go(embq.at[cut_q[h]], allq_ref.at[q, cut_q[h]], row[d]) for h in (d, 1 - d)]
-    keep(embq, allq_ref.at[q])
-    embp[...] = acc[pl.ds(rows, rows)].astype(jnp.bfloat16)
-    keep(embp, embp_ref)
-    keep(w_buf, full_ref)
+        q_near[d] = [go(q_buf.at[q, cut_q[h]], q_buf.at[q, cut_q[h]], row[d]) for h in (d, 1 - d)]
+    p_buf[...] = acc[1].astype(jnp.bfloat16)
+    keep_w = keep(w_buf, full_ref)
     for copy in list_copies:
         copy.wait_recv()
-    lists_ref[...] = list_buf[...]
+    take_index = keep(list_buf, index_buf)
+    inner[...] = scale * lax.dot_general(
+        q_buf[q], p_buf[...], (((1,), (1,)), ((), ())), preferred_element_type=jnp.float32
+    )
+    take_index.wait()
+    keep_w.wait()
+    for copy in w_sent:
+        copy.wait_send()
     q_far = [None, None]
     for d in range(2):
         came = wrap(q - 1 + 2 * d)
         q_near[d][0].wait_recv()
-        q_far[d] = go(allq_ref.at[came, cut_q[d]], allq_ref.at[came, cut_q[d]], row[d])
+        q_far[d] = go(q_buf.at[came, cut_q[d]], q_buf.at[came, cut_q[d]], row[d])
+    take_b.wait()
     for d in range(2):
         b_near[d][1].wait_recv()
         b_far[d].wait_recv()
-        q_near[d][1].wait_recv()
-        q_far[d].wait_recv()
-    for copy in local[3:]:
-        copy.wait()
-    for copy in started:
-        copy.wait_send()
-
-
-def gather_and_embed(queries, passages, weight, bank, lists):
-    rows, features = queries.shape
-    depth, width = weight.shape
-    parts = features // depth
-    many, block_rows = bank.shape[:2]
-    anywhere = pl.BlockSpec(memory_space=pltpu.HBM)
-    vmem = pl.BlockSpec(memory_space=pltpu.VMEM)
-    return pl.pallas_call(
-        gather_kernel,
-        out_shape=(
-            jax.ShapeDtypeStruct((RING, many, block_rows, width), jnp.bfloat16),
-            jax.ShapeDtypeStruct((RING, rows, width), jnp.bfloat16),
-            jax.ShapeDtypeStruct((rows, width), jnp.bfloat16),
-            jax.ShapeDtypeStruct((parts, depth, width), jnp.bfloat16),
-            jax.ShapeDtypeStruct((2, features // 2, 2 * rows), jnp.bfloat16),
-            jax.ShapeDtypeStruct(lists.shape, jnp.int32),
-        ),
-        in_specs=[anywhere] * 4 + [vmem],
-        out_specs=(anywhere,) * 5 + (vmem,),
-        scratch_shapes=[
-            pltpu.VMEM((parts, depth, width), jnp.bfloat16),
-            pltpu.VMEM((2 * rows, features), jnp.bfloat16),
-            pltpu.VMEM((2, features // 2, 2 * rows), jnp.bfloat16),
-            pltpu.VMEM((2 * rows, width), jnp.float32),
-            pltpu.VMEM((rows, width), jnp.bfloat16),
-            pltpu.VMEM((rows, width), jnp.bfloat16),
-            pltpu.VMEM(lists.shape, jnp.int32),
-            pltpu.SemaphoreType.DMA((8,)),
-            pltpu.SemaphoreType.DMA((28,)),
-            pltpu.SemaphoreType.DMA((28,)),
-        ],
-        compiler_params=pltpu.CompilerParams(
-            collective_id=0, has_side_effects=True, vmem_limit_bytes=40 * 1024 * 1024
-        ),
-        name="gather_and_embed",
-    )(queries, passages, weight, bank, lists)
-
-
-NONE = -1e30
-
-
-def partial_kernel(
-    scale, allq_ref, blocks_ref, embp_ref, index_ref, list_ref,
-    grad_ref, loss_ref,
-    q_buf, x_buf, p_buf, named, prob, score, mixed, own_mixed,
-    far_out, near_out, passing, arriving,
-    far_stat, near_stat, pass_stat, arrive_stat, arrive_far, local_sem, send, recv,
-):
-    r, q, x, core = ring_position()
-    row = [ring_device(r, q + by, x, core) for by in (1, -1)]
-    rows, width = p_buf.shape
-    places = list_ref.shape[1]
-    half = width // 2
-    sides = (pl.ds(0, half), pl.ds(half, half))
-
-    take = [
-        pltpu.make_async_copy(allq_ref, q_buf, local_sem.at[0]),
-        pltpu.make_async_copy(blocks_ref, x_buf, local_sem.at[1]),
-        pltpu.make_async_copy(embp_ref, p_buf, local_sem.at[2]),
-    ]
-    for copy in take:
-        copy.start()
-    greet(row)
-    for copy in take:
-        copy.wait()
-
-    def wrap(v):
-        return lax.rem(v + RING, RING)
-
-    started = []
-
-    def go(src, dst, target):
-        n = len(started)
-        copy = remote(src, dst, send.at[n], recv.at[n], target)
-        copy.start()
-        started.append(copy)
-        return copy
 
     eye = lax.broadcasted_iota(jnp.int32, (128, 128), 0) == lax.broadcasted_iota(jnp.int32, (128, 128), 1)
 
@@ -548,77 +489,96 @@
     def unpack(stat, n):
         parts = []
         for i in range(rows // 128):
-            line = stat[pl.ds(n * (rows // 128) + i, 1)]
-            parts.append(jnp.sum(jnp.where(eye, line, 0.0), axis=1, keepdims=True))
+            one = stat[pl.ds(n * (rows // 128) + i, 1)]
+            parts.append(jnp.sum(jnp.where(eye, one, 0.0), axis=1, keepdims=True))
         return jnp.concatenate(parts, axis=0)
 
-    def group(g, result):
-        @pl.loop(0, places)
-        def _(k):
-            block = jnp.maximum(index_ref[g, k, 0], 0)
-            named[pl.ds(pl.multiple_of(k * 128, 128), 128)] = x_buf[block]
-
+    def group(g):
         @pl.loop(0, places // 2)
         def _(n):
+            for k in range(2):
+                block = jnp.maximum(index_buf[g, 2 * n + k, 0], 0)
+                w_buf[n, k * 128 : (k + 1) * 128] = x_buf[block]
             part = pl.ds(pl.multiple_of(n * 256, 256), 256)
             score[:, part] = scale * lax.dot_general(
-                q_buf[g], named[part], (((1,), (1,)), ((), ())), preferred_element_type=jnp.float32
+                q_buf[g], w_buf[n], (((1,), (1,)), ((), ())), preferred_element_type=jnp.float32
             )
 
         top = jnp.full((rows, 128), NONE, jnp.float32)
         for k in range(places):
-            valid = list_ref[g, pl.ds(k, 1)] >= 0
+            valid = list_buf[g, pl.ds(k, 1)] >= 0
             top = jnp.maximum(top, jnp.where(valid, score[:, k * 128 : (k + 1) * 128], NONE))
         m = jnp.max(top, axis=1, keepdims=True)
         total = jnp.zeros((rows, 128), jnp.float32)
         for k in range(places):
-            valid = list_ref[g, pl.ds(k, 1)] >= 0
+            valid = list_buf[g, pl.ds(k, 1)] >= 0
             e = jnp.where(valid, jnp.exp(score[:, k * 128 : (k + 1) * 128] - m), 0.0)
             total = total + e
             prob[:, k * 128 : (k + 1) * 128] = e.astype(jnp.bfloat16)
-        l = jnp.sum(total, axis=1, keepdims=True)
-
-        @pl.loop(0, width // 512)
-        def _(n):
-            part = pl.ds(pl.multiple_of(n * 512, 512), 512)
-            result[:, part] = jnp.dot(prob[...], named[:, part], preferred_element_type=jnp.float32)
-
-        return m, l
-
-    m, l = group(wrap(q + 2), mixed)
+        return m, jnp.sum(total, axis=1, keepdims=True)
+
+    def weighted(n):
+        named = w_buf[pl.ds(0, places // 2), :, pl.ds(n * TILE, TILE)]
+        return jnp.dot(prob[...], named.reshape(places * 128, TILE), preferred_element_type=jnp.float32)
+
+    tiles = half // TILE
+    m_near = [None, None]
+    stats = []
+    plain = [None, None]
+
+    def near_group(d):
+        q_near[1 - d][1].wait_recv()
+        m_near[d], l = group(wrap(q + 1 - 2 * d))
+        pack(near_stat.at[d], m_near[d], l)
+        stats.append(go(near_stat.at[d], arrive_stat.at[d], row[d]))
+        for t in range(tiles):
+            near_out[d, 1 - d, t] = weighted((1 - d) * tiles + t).astype(jnp.bfloat16)
+        plain[d] = go(near_out.at[d, 1 - d], arriving.at[d, 1 - d], row[d])
+        for t in range(tiles):
+            n = d * tiles + t
+            acc[1, :, n * TILE : (n + 1) * TILE] = weighted(n)
+
+    m_own, l_own = group(q)
+    for n in range(2 * tiles):
+        acc[0, :, n * TILE : (n + 1) * TILE] = weighted(n)
+    near_group(0)
+
+    for copy in q_far:
+        copy.wait_recv()
+    m, l = group(wrap(q + 2))
     pack(far_stat, m, l)
-    far = []
+    far_stats = [go(far_stat, pass_stat.at[d], row[d]) for d in range(2)]
+    far = [[], []]
+    for t in range(tiles):
+        for d in range(2):
+            far_out[d, t] = weighted(d * tiles + t).astype(jnp.bfloat16)
+            far[d].append(go(far_out.at[d, t], passing.at[d, t], row[d]))
+    near_group(1)
+
+    m_in = jnp.max(inner[...], axis=1, keepdims=True)
+    l_in = jnp.sum(jnp.exp(inner[...] - m_in), axis=1, keepdims=True)
+    diagonal = lax.broadcasted_iota(jnp.int32, inner.shape, 0) == lax.broadcasted_iota(jnp.int32, inner.shape, 1)
+    positive = jnp.sum(jnp.where(diagonal, inner[...], 0.0), axis=1, keepdims=True)
+
+    by_near, by_far = [], []
     for d in range(2):
-        far_out[d] = mixed[:, sides[d]].astype(jnp.bfloat16)
-        far.append(
-            (go(far_out.at[d], passing.at[d], row[d]), go(far_stat, pass_stat.at[d], row[d]))
-        )
-    near = []
-    for d in range(2):
-        m, l = group(wrap(q + 1 - 2 * d), mixed)
-        pack(near_stat.at[d], m, l)
-        for copy in far[d]:
-            copy.wait_recv()
+        far_stats[d].wait_recv()
+        if d == 0:
+            stats.append(go(pass_stat.at[0], arrive_far, row[0]))
         m_far = unpack(pass_stat.at[d], 0)
-        both = jnp.maximum(m, m_far)
-        joined = mixed[:, sides[d]] * jnp.exp(m - both) + passing[d].astype(jnp.float32) * jnp.exp(m_far - both)
-        near_out[d, :, sides[d]] = joined.astype(jnp.bfloat16)
-        near_out[d, :, sides[1 - d]] = mixed[:, sides[1 - d]].astype(jnp.bfloat16)
-        near.append(go(near_out.at[d], arriving.at[d], row[d]))
-        near.append(go(near_stat.at[d], arrive_stat.at[d], row[d]))
-        if d == 0:
-            near.append(go(pass_stat.at[0], arrive_far, row[0]))
-
-    m_own, l_own = group(q, own_mixed)
-    inner = scale * lax.dot_general(
-        q_buf[q], p_buf[...], (((1,), (1,)), ((), ())), preferred_element_type=jnp.float32
-    )
-    m_in = jnp.max(inner, axis=1, keepdims=True)
-    l_in = jnp.sum(jnp.exp(inner - m_in), axis=1, keepdims=True)
-    diagonal = lax.broadcasted_iota(jnp.int32, inner.shape, 0) == lax.broadcasted_iota(jnp.int32, inner.shape, 1)
-    positive = jnp.sum(jnp.where(diagonal, inner, 0.0), axis=1, keepdims=True)
-
-    for copy in near:
+        both = jnp.maximum(m_near[d], m_far)
+        by_near.append(jnp.exp(m_near[d] - both))
+        by_far.append(jnp.exp(m_far - both))
+    joined = [[], []]
+    for t in range(tiles):
+        for d in range(2):
+            n = d * tiles + t
+            far[d][t].wait_recv()
+            value = acc[1, :, n * TILE : (n + 1) * TILE] * by_near[d] + passing[d, t].astype(jnp.float32) * by_far[d]
+            near_out[d, d, t] = value.astype(jnp.bfloat16)
+            joined[d].append(go(near_out.at[d, d, t], arriving.at[d, d, t], row[d]))
+
+    for copy in stats:
         copy.wait_recv()
     m_before, l_before = unpack(arrive_stat.at[0], 0), unpack(arrive_stat.at[0], 1)
     m_after, l_after = unpack(arrive_stat.at[1], 0), unpack(arrive_stat.at[1], 1)
@@ -632,8 +592,14 @@
     losses = m + jnp.log(total) - positive
     loss_ref[...] = jnp.broadcast_to(jnp.sum(losses, axis=0, keepdims=True), loss_ref.shape)
     target = jnp.where(diagonal, 1.0, 0.0)
-    grad_full = (jnp.exp(inner - m) / total - target) * scale
+    grad_full = (jnp.exp(inner[...] - m) / total - target) * scale
     grad_in = grad_full.astype(jnp.bfloat16)
+    turned = grad_full.T.astype(jnp.bfloat16)
+    for n in range(width // 512):
+        part = pl.ds(n * 512, 512)
+        value = jnp.dot(turned, q_buf[q, :, part], preferred_element_type=jnp.float32)
+        h_buf[pl.ds(rows, rows), part] = value.astype(jnp.bfloat16)
+    keep(h_buf.at[pl.ds(rows, rows)], grad_ref.at[pl.ds(rows, rows)])
     by_own = jnp.exp(m_own - m) * (scale / total)
     by_before = (
         jnp.exp(jnp.maximum(m_before, m_far) - m) * (scale / total),
@@ -643,66 +609,77 @@
         jnp.exp(m_after - m) * (scale / total),
         jnp.exp(jnp.maximum(m_after, m_far) - m) * (scale / total),
     )
-    for n in range(width // 512):
-        part = pl.ds(n * 512, 512)
-        side = n * 512 // half
-        value = jnp.dot(grad_in, p_buf[:, part], preferred_element_type=jnp.float32)
-        value = value + own_mixed[:, part] * by_own
-        value = value + arriving[0, :, part].astype(jnp.float32) * by_before[side]
-        value = value + arriving[1, :, part].astype(jnp.float32) * by_after[side]
-        grad_ref[pl.ds(0, rows), part] = value.astype(jnp.bfloat16)
-    turned = grad_full.T.astype(jnp.bfloat16)
-    for n in range(width // 512):
-        part = pl.ds(n * 512, 512)
-        value = jnp.dot(turned, q_buf[q, :, part], preferred_element_type=jnp.float32)
-        grad_ref[pl.ds(rows, rows), part] = value.astype(jnp.bfloat16)
+    for copy in plain:
+        copy.wait_recv()
+    for t in range(tiles):
+        for side in range(2):
+            joined[side][t].wait_recv()
+            part = pl.ds((side * tiles + t) * TILE, TILE)
+            value = jnp.dot(grad_in, p_buf[:, part], preferred_element_type=jnp.float32)
+            value = value + acc[0, :, part] * by_own
+            value = value + arriving[0, side, t].astype(jnp.float32) * by_before[side]
+            value = value + arriving[1, side, t].astype(jnp.float32) * by_after[side]
+            h_buf[pl.ds(0, rows), part] = value.astype(jnp.bfloat16)
+    keep(h_buf.at[pl.ds(0, rows)], grad_ref.at[pl.ds(0, rows)])
+    for copy in local:
+        if not any(copy is c for c in (take_q, take_p, take_w, take_b, take_index, keep_w)):
+            copy.wait()
     for copy in started:
-        copy.wait_send()
-
-
-def embedding_gradients(scale, all_q, blocks, emb_p, lists):
-    rows, width = emb_p.shape
-    count, block_rows = blocks.shape[0] * blocks.shape[1], blocks.shape[2]
-    blocks = blocks.reshape(count, block_rows, width)
+        if not any(copy is c for c in w_sent):
+            copy.wait_send()
+
+
+def embedding_gradients(scale, queries, passages, weight, bank, lists):
+    rows, features = queries.shape
+    depth, width = weight.shape
+    parts = features // depth
+    many, block_rows = bank.shape[:2]
     places = lists.shape[1]
-    anywhere = pl.BlockSpec(memory_space=pltpu.HBM)
+    half = width // 2
+    bf16, f32 = jnp.bfloat16, jnp.float32
+    hbm = pl.BlockSpec(memory_space=pltpu.HBM)
     vmem = pl.BlockSpec(memory_space=pltpu.VMEM)
-    bf16, f32 = jnp.bfloat16, jnp.float32
     return pl.pallas_call(
-        lambda *refs: partial_kernel(scale, *refs),
+        lambda *refs: embed_kernel(scale, *refs),
         out_shape=(
+            jax.ShapeDtypeStruct((parts, depth, width), bf16),
+            jax.ShapeDtypeStruct((2, features // 2, 2 * rows), bf16),
             jax.ShapeDtypeStruct((2 * rows, width), bf16),
             jax.ShapeDtypeStruct((8, 128), f32),
         ),
-        in_specs=[anywhere] * 3 + [pl.BlockSpec(memory_space=pltpu.SMEM), vmem],
-        out_specs=(vmem, vmem),
+        in_specs=[hbm] * 4 + [vmem],
+        out_specs=(hbm, hbm, hbm, vmem),
         scratch_shapes=[
-            pltpu.VMEM(all_q.shape, bf16),
-            pltpu.VMEM(blocks.shape, bf16),
+            pltpu.VMEM((parts, depth, width), bf16),
+            pltpu.VMEM((2 * rows, features), bf16),
+            pltpu.VMEM((2, features // 2, 2 * rows), bf16),
+            pltpu.VMEM((2, rows, width), f32),
+            pltpu.VMEM((RING, rows, width), bf16),
+            pltpu.VMEM((RING * many, block_rows, width), bf16),
             pltpu.VMEM((rows, width), bf16),
-            pltpu.VMEM((places * block_rows, width), bf16),
             pltpu.VMEM((rows, places * block_rows), bf16),
             pltpu.VMEM((rows, places * block_rows), f32),
-            pltpu.VMEM((rows, width), f32),
-            pltpu.VMEM((rows, width), f32),
-            pltpu.VMEM((2, rows, width // 2), bf16),
-            pltpu.VMEM((2, rows, width), bf16),
-            pltpu.VMEM((2, rows, width // 2), bf16),
-            pltpu.VMEM((2, rows, width), bf16),
+            pltpu.VMEM((rows, rows), f32),
+            pltpu.VMEM((2, half // TILE, rows, TILE), bf16),
+            pltpu.VMEM((2, 2, half // TILE, rows, TILE), bf16),
+            pltpu.VMEM((2, half // TILE, rows, TILE), bf16),
+            pltpu.VMEM((2, 2, half // TILE, rows, TILE), bf16),
             pltpu.VMEM((8, 128), f32),
             pltpu.VMEM((2, 8, 128), f32),
             pltpu.VMEM((2, 8, 128), f32),
             pltpu.VMEM((2, 8, 128), f32),
             pltpu.VMEM((8, 128), f32),
-            pltpu.SemaphoreType.DMA((3,)),
+            pltpu.VMEM(lists.shape, jnp.int32),
+            pltpu.SMEM(lists.shape, jnp.int32),
             pltpu.SemaphoreType.DMA((9,)),
-            pltpu.SemaphoreType.DMA((9,)),
+            pltpu.SemaphoreType.DMA((43,)),
+            pltpu.SemaphoreType.DMA((43,)),
         ],
         compiler_params=pltpu.CompilerParams(
-            collective_id=1, has_side_effects=True, vmem_limit_bytes=60 * 1024 * 1024
+            collective_id=0, has_side_effects=True, vmem_limit_bytes=VMEM_LIMIT
         ),
         name="embedding_gradients",
-    )(all_q, blocks, emb_p, lists, lists)
+    )(queries, passages, weight, bank, lists)
 
 
 def body(queries, passages, weight, bank, neg_ids, block_home):
@@ -730,8 +707,9 @@
     lists = jnp.sum(jnp.where(hit, block[:, None, None] + 1, 0), axis=0) - 1
     lists = jnp.broadcast_to(lists[:, :, None], lists.shape + (128,))
 
-    blocks, all_q, emb_p, full_weight, turned, all_lists = gather_and_embed(queries, passages, weight, bank, lists)
-    grad_rows, loss_local = embedding_gradients(logit_scale, all_q, blocks, emb_p, all_lists)
+    full_weight, turned, grad_rows, loss_local = embedding_gradients(
+        logit_scale, queries, passages, weight, bank, lists
+    )
     grad_weight, losses, back_q, back_p = reduce_gradient(turned, grad_rows, full_weight, loss_local)
     loss = losses[0, 0] / (count_q * n_dp * n_fsdp)
     return (loss, grad_weight, back_q, back_p)

time: 223 us -> 201 us (0.901)
  Pallas kernels: 204 us -> 191 us
  local copies, waits for them, and re-layouts: 14.4 us -> 5.45 us
    pallas_call x2 -> x1, Pallas kernels: 159 us -> 147 us  [embedding_gradients(): pl.pallas_call(lambda *refs: embed_kernel(scale, *refs), out_shape=(jax.S...]
    unnamed x21 -> x7, local copies, waits for them, and re-layouts: 13.2 us -> 3.62 us
where the time goes in v4:
time: 201 us; the launch traced here: 200 us
  Pallas kernels  191 us (95%)
  local copies, waits for them, and re-layouts  5.45 us (3%)
  between operations  2.49 us (1%)
    pallas_call x1, Pallas kernels, embedding_gradients(): pl.pallas_call(lambda *refs: embed_kernel(scale, *refs), out_shape=(jax.S...  147 us
    pallas_call x1, Pallas kernels, reduce_gradient(): pl.pallas_call(reduce_kernel, out_shape=(jax.ShapeDtypeStruct((ROWS, widt...  43.9 us

profile of v4, /device:TPU:0, one launch (start us, length us, event | category | flops | bytes accessed | tf_op | source)
XLA Modules:
  0.0 200.3 jit_solution(5883924567637188462)
XLA Ops:
  0.6 0.0 copy-start
  0.7 0.7 fusion.3
  1.3 0.0 copy-done
  1.3 0.6 gather_fusion
  2.0 0.2 convert_reduce_fusion
  2.2 0.1 select_reduce_fusion
  2.4 0.7 broadcast_in_dim.12.refs_4_
  3.1 147.5 %embedding_gradients.1 = (bf16[8,256,2048]{2,1,0:T(8,128)(2,1)}, bf16[2,1024,768]{2,1,0:T(8,128)(2,1)}, bf16[768,2048]{1,0:T(8,128)(2,1)}, f32[8,128]{1,0:T(8,128)}) custom-call(bf16[384,2048]{1,0:T(8,128)(2,1)} %refs_0_.1, bf16[384,2048]{1,0:T(8,128)(2,1)} %refs_1_.1, bf16[256,2048]{1,0:T(8,128)(2,1)} %refs_2_.1, bf16[8,128,2048]{2,1,0:T(8,128)(2,1)} %refs_3_.1, ...), custom_call_target="tpu_custom_call" | custom-call | tf_op jit(solution)/shard_map/embedding_gradients/pallas_call | solution.py:642
  150.5 0.0 copy-start.1
  150.5 0.7 copy-done.1
  151.2 43.9 %reduce_gradient.1 = (f32[16,2048]{1,0:T(8,128)S(1)}, f32[8,128]{1,0:T(8,128)S(1)}, bf16[384,2048]{1,0:T(8,128)(2,1)S(1)}, bf16[384,2048]{1,0:T(8,128)(2,1)S(1)}) custom-call(bf16[2,1024,768]{2,1,0:T(8,128)(2,1)} %get-tuple-element.12.turned_ref, bf16[768,2048]{1,0:T(8,128)(2,1)} %get-tuple-element.13.rows_ref, ...), custom_call_target="tpu_custom_call" | custom-call | tf_op jit(solution)/shard_map/reduce_gradient/pallas_call | solution.py:288
  195.1 0.5 slice.3
  196.2 0.7 copy.13
  196.9 1.1 copy.14
  198.0 1.1 copy.15
  (6 shorter events, 0.1 us)
Async XLA Ops:
  0.6 0.7 copy-start
  150.5 0.7 copy-start.1

commit v5 on v4

--- a/solution.py
+++ b/solution.py
@@ -453,9 +453,6 @@
     multiply(last + 1 - core)
 
     q_buf[pl.ds(q, 1)] = acc[pl.ds(0, 1)].astype(jnp.bfloat16)
-    q_near = [None, None]
-    for d in range(2):
-        q_near[d] = [go(q_buf.at[q, cut_q[h]], q_buf.at[q, cut_q[h]], row[d]) for h in (d, 1 - d)]
     p_buf[...] = acc[1].astype(jnp.bfloat16)
     keep_w = keep(w_buf, full_ref)
     for copy in list_copies:
@@ -468,11 +465,11 @@
     keep_w.wait()
     for copy in w_sent:
         copy.wait_send()
-    q_far = [None, None]
-    for d in range(2):
-        came = wrap(q - 1 + 2 * d)
-        q_near[d][0].wait_recv()
-        q_far[d] = go(q_buf.at[came, cut_q[d]], q_buf.at[came, cut_q[d]], row[d])
+    for copy in b_far:
+        copy.wait_send()
+    q_near = [[], []]
+    for d in range(2):
+        q_near[d].append(go(q_buf.at[q, cut_q[d]], q_buf.at[q, cut_q[d]], row[d]))
     take_b.wait()
     for d in range(2):
         b_near[d][1].wait_recv()
@@ -539,9 +536,17 @@
             acc[1, :, n * TILE : (n + 1) * TILE] = weighted(n)
 
     m_own, l_own = group(q)
+    for d in range(2):
+        q_near[d].append(go(q_buf.at[q, cut_q[1 - d]], q_buf.at[q, cut_q[1 - d]], row[d]))
     for n in range(2 * tiles):
         acc[0, :, n * TILE : (n + 1) * TILE] = weighted(n)
+    q_far = [None, None]
+    for d in range(2):
+        came = wrap(q - 1 + 2 * d)
+        q_near[d][0].wait_recv()
+        q_far[d] = go(q_buf.at[came, cut_q[d]], q_buf.at[came, cut_q[d]], row[d])
     near_group(0)
+    near_group(1)
 
     for copy in q_far:
         copy.wait_recv()
@@ -553,7 +558,6 @@
         for d in range(2):
             far_out[d, t] = weighted(d * tiles + t).astype(jnp.bfloat16)
             far[d].append(go(far_out.at[d, t], passing.at[d, t], row[d]))
-    near_group(1)
 
     m_in = jnp.max(inner[...], axis=1, keepdims=True)
     l_in = jnp.sum(jnp.exp(inner[...] - m_in), axis=1, keepdims=True)
@@ -625,7 +629,7 @@
         if not any(copy is c for c in (take_q, take_p, take_w, take_b, take_index, keep_w)):
             copy.wait()
     for copy in started:
-        if not any(copy is c for c in w_sent):
+        if not any(copy is c for c in w_sent + b_far):
             copy.wait_send()
 
 

time: 201 us -> 189 us (0.940)
  Pallas kernels: 191 us -> 180 us
    pallas_call x1, Pallas kernels: 147 us -> 135 us  [embedding_gradients(): pl.pallas_call(lambda *refs: embed_kernel(scale, *refs), out_shape=(jax.S...]
where the time goes in v5:
time: 189 us
  Pallas kernels  180 us (95%)
  local copies, waits for them, and re-layouts  5.45 us (3%)
  between operations  2.49 us (1%)
    pallas_call x1, Pallas kernels, embedding_gradients(): pl.pallas_call(lambda *refs: embed_kernel(scale, *refs), out_shape=(jax.S...  135 us
    pallas_call x1, Pallas kernels, reduce_gradient(): pl.pallas_call(reduce_kernel, out_shape=(jax.ShapeDtypeStruct((ROWS, widt...  45.4 us

profile of v5, /device:TPU:0, one launch (start us, length us, event | category | flops | bytes accessed | tf_op | source)
XLA Modules:
  0.0 189.0 jit_solution(1710592783997963503)
XLA Ops:
  0.6 0.0 copy-start
  0.7 0.7 fusion.3
  1.3 0.0 copy-done
  1.3 0.6 gather_fusion
  2.0 0.2 convert_reduce_fusion
  2.2 0.1 select_reduce_fusion
  2.4 0.7 broadcast_in_dim.12.refs_4_
  3.1 134.6 %embedding_gradients.1 = (bf16[8,256,2048]{2,1,0:T(8,128)(2,1)}, bf16[2,1024,768]{2,1,0:T(8,128)(2,1)}, bf16[768,2048]{1,0:T(8,128)(2,1)}, f32[8,128]{1,0:T(8,128)}) custom-call(bf16[384,2048]{1,0:T(8,128)(2,1)} %refs_0_.1, bf16[384,2048]{1,0:T(8,128)(2,1)} %refs_1_.1, bf16[256,2048]{1,0:T(8,128)(2,1)} %refs_2_.1, bf16[8,128,2048]{2,1,0:T(8,128)(2,1)} %refs_3_.1, ...), custom_call_target="tpu_custom_call" | custom-call | tf_op jit(solution)/shard_map/embedding_gradients/pallas_call | solution.py:646
  137.7 0.0 copy-start.1
  137.7 0.7 copy-done.1
  138.3 45.4 %reduce_gradient.1 = (f32[16,2048]{1,0:T(8,128)S(1)}, f32[8,128]{1,0:T(8,128)S(1)}, bf16[384,2048]{1,0:T(8,128)(2,1)S(1)}, bf16[384,2048]{1,0:T(8,128)(2,1)S(1)}) custom-call(bf16[2,1024,768]{2,1,0:T(8,128)(2,1)} %get-tuple-element.12.turned_ref, bf16[768,2048]{1,0:T(8,128)(2,1)} %get-tuple-element.13.rows_ref, ...), custom_call_target="tpu_custom_call" | custom-call | tf_op jit(solution)/shard_map/reduce_gradient/pallas_call | solution.py:288
  183.7 0.5 slice.3
  184.9 0.7 copy.13
  185.5 1.1 copy.14
  186.7 1.1 copy.15
  (6 shorter events, 0.1 us)
Async XLA Ops:
  0.6 0.7 copy-start
  137.7 0.7 copy-start.1
